TPU v7x, 128 devices: a whole 4x4x4 slice. The times are simulated.
128 devices in a mesh: dp: 8 (over y_hi, z), tensor: 16 (over y_lo, x, core).
Axes of the slice: x: 4, y: 4 (y_hi: 2, y_lo: 2; y = y_hi * 2 + y_lo), z: 4, core: 2. Of those that a mesh axis runs over, the one named last changes fastest.
Arguments:
- inputs: bfloat16 [8192, 5120], P(('dp', 'tensor')), may hold values from -24 to 24
- norm_gain: float32 [5120], replicated, may hold values from 0.5 to 1.5
- w_in: bfloat16 [5120, 20480], P(None, 'tensor'), may hold values from -0.078125 to 0.078125
- pre_gelu: bfloat16 [8192, 20480], P('dp', 'tensor'), may hold values from -6 to 6
- grad_hidden: bfloat16 [8192, 20480], P('dp', 'tensor'), may hold values from -6 to 6
- grad_out: bfloat16 [8192, 5120], P(('dp', 'tensor')), may hold values from -6 to 6
Outputs:
- grad_in: bfloat16 [8192, 5120], P(('dp', 'tensor'))
- grad_w_in: bfloat16 [5120, 20480], P('dp', 'tensor')
All inputs are finite; a program needn't handle non-finite values.
Results may differ from a plain program's by a relative error of at most 0.02.
Values may be sent and summed in bfloat16 or wider, within the bound.
No kernel may reach another device: no remote copies, remote signals or barrier semaphores. Data moves between devices by JAX's collectives and lax.ppermute only.
A program may use at most 128 MiB of HBM per device.

v0:
```python
import jax
import jax.numpy as jnp
from jax import lax
from jax.sharding import PartitionSpec as P


def normalize(row_block):
    values = row_block.astype(jnp.float32)
    center = jnp.mean(values, axis=1, keepdims=True)
    shifted = values - center
    variance = jnp.mean(shifted * shifted, axis=1, keepdims=True)
    inv_std = lax.rsqrt(variance + 1e-05)
    return (shifted * inv_std, inv_std)


def gelu_slope(pre_vals):
    tanh_arg = 0.7978845608 * (pre_vals + 0.044715 * pre_vals * pre_vals * pre_vals)
    tangent = jnp.tanh(tanh_arg)
    return 0.5 * (1.0 + tangent) + 0.5 * pre_vals * (1.0 - tangent * tangent) * 0.7978845608 * (
        1.0 + 3.0 * 0.044715 * pre_vals * pre_vals
    )


def local(inputs, norm_gain, w_in, pre_gelu, grad_hidden, grad_out):
    unit_rows, inv_std = normalize(inputs)
    grad_pre = (grad_hidden.astype(jnp.float32) * gelu_slope(pre_gelu.astype(jnp.float32))).astype(
        jnp.bfloat16
    )
    outgoing = (unit_rows * norm_gain).astype(jnp.bfloat16)
    normed_all = lax.all_gather(outgoing, "tensor", axis=0, tiled=True)
    partial_value = lax.dot_general(
        normed_all, grad_pre, (((0,), (0,)), ((), ())), preferred_element_type=jnp.float32
    )
    weight_total = lax.psum_scatter(
        partial_value.astype(jnp.bfloat16), "dp", scatter_dimension=0, tiled=True
    )
    grad_normed = lax.psum_scatter(
        lax.dot_general(
            grad_pre, w_in, (((1,), (1,)), ((), ())), preferred_element_type=jnp.float32
        ).astype(jnp.bfloat16),
        "tensor",
        scatter_dimension=0,
        tiled=True,
    ).astype(jnp.float32)
    scaled = grad_normed * norm_gain
    grad_norm = inv_std * (
        scaled
        - jnp.mean(scaled, axis=1, keepdims=True)
        - unit_rows * jnp.mean(scaled * unit_rows, axis=1, keepdims=True)
    )
    grad_in = (grad_out.astype(jnp.float32) + grad_norm).astype(jnp.bfloat16)
    return (grad_in, weight_total)


def solution(mesh):
    placed = (
        P(("dp", "tensor"), None),
        P(),
        P(None, "tensor"),
        P("dp", "tensor"),
        P("dp", "tensor"),
        P(("dp", "tensor"), None),
    )
    return jax.shard_map(
        local,
        mesh=mesh,
        in_specs=placed,
        out_specs=(P(("dp", "tensor"), None), P("dp", "tensor")),
        check_vma=False,
    )
```

profile of v0, /device:TPU:0, one launch (start us, length us, event | category | flops | bytes accessed | tf_op | source)
XLA Modules:
  0.0 363.9 jit_solution(18035494318364750684)
XLA Ops:
  7.2 0.0 reduce-scatter.3.cloned.1.call-start
  7.2 25.3 %convolution_convert_fusion.1 = bf16[1024,5120]{1,0:T(8,128)(2,1)} fusion(bf16[5120,1280]{1,0:T(8,128)(2,1)} %param.8, bf16[1024,1280]{1,0:T(8,128)(2,1)} %param.9, bf16[1024,1280]{1,0:T(8,128)(2,1)} %param.10), kind=kOutput, calls=%fused_computation.8 | convolution fusion | flops 13454540800 | bytes 28835840 | tf_op jit(solution)/shard_map/dot_general | solution.py:38
  32.5 0.0 copy-start
  32.5 0.0 copy-start.2
  32.5 0.0 copy-start.1
  32.5 0.0 reduce-scatter.3.cloned.1.call-update
  32.6 0.0 all-gather.2.cloned.1.call-start
  32.6 1.0 copy-done
  33.6 0.2 convert_reduce_fusion
  33.8 0.3 fusion.20
  34.2 79.5 %reduce-scatter.3.cloned.1.call-done = bf16[64,5120]{1,0:T(8,128)(2,1)} async-done(((bf16[1024,5120]{1,0:T(8,128)(2,1)}), bf16[64,5120]{1,0:T(8,128)(2,1)}) %reduce-scatter.3.cloned.1.call-update) | async-done | bytes 655376 | tf_op jit(solution)/shard_map/reduce_scatter | solution.py:37
  113.7 0.0 copy-done.2
  113.7 1.5 fusion.21
  115.2 0.0 copy-done.1
  115.2 2.7 fusion.19
  118.0 0.0 all-gather.2.cloned.1.call-update
  118.0 0.2 reduce-scatter.5.cloned.1.call-start
  118.2 60.7 %all-gather.2.cloned.1.call-done = bf16[1024,5120]{1,0:T(8,128)(2,1)} async-done(((bf16[64,5120]{1,0:T(8,128)(2,1)}), bf16[1024,5120]{1,0:T(8,128)(2,1)}) %all-gather.2.cloned.1.call-update) | async-done | bytes 10485776 | tf_op jit(solution)/shard_map/all_gather | solution.py:30
  179.0 21.6 %convolution_convert_fusion = bf16[5120,1280]{1,0:T(8,128)(2,1)} fusion(bf16[1024,5120]{1,0:T(8,128)(2,1)} %all-gather.2.cloned.1.call-done, bf16[1024,1280]{1,0:T(8,128)(2,1)} %param.9, bf16[1024,1280]{1,0:T(8,128)(2,1)} %param.10), kind=kOutput, calls=%fused_computation | convolution fusion | flops 13455851520 | bytes 28835840 | tf_op jit(solution)/shard_map/dot_general | solution.py:31
  200.5 0.0 reduce-scatter.5.cloned.1.call-update
  200.6 156.8 %reduce-scatter.5.cloned.1.call-done = bf16[640,1280]{1,0:T(8,128)(2,1)} async-done(((bf16[5120,1280]{1,0:T(8,128)(2,1)}), bf16[640,1280]{1,0:T(8,128)(2,1)}) %reduce-scatter.5.cloned.1.call-update) | async-done | bytes 1638416 | tf_op jit(solution)/shard_map/reduce_scatter | solution.py:34
  (3 shorter events, 0.0 us)
Async XLA Ops:
  7.2 106.5 %reduce-scatter.3.cloned.1.call-start = ((), (), s32[]{:S(2)}) async-start(), calls=%async_computation.2 | async-start | bytes 11141120 | tf_op jit(solution)/shard_map/reduce_scatter | solution.py:37
  32.5 1.1 copy-start
  32.5 81.1 %copy-start.2 = (f32[5120]{0:T(1024)S(1)}, f32[5120]{0:T(1024)}, u32[]{:S(2)}) copy-start(f32[5120]{0:T(1024)} %param.7) | copy-start | bytes 61444
  32.5 82.7 %copy-start.1 = (bf16[64,5120]{1,0:T(8,128)(2,1)S(1)}, bf16[64,5120]{1,0:T(8,128)(2,1)}, u32[]{:S(2)}) copy-start(bf16[64,5120]{1,0:T(8,128)(2,1)} %param.11) | copy-start | bytes 1966084
  32.6 146.4 %all-gather.2.cloned.1.call-start = ((), (), s32[]{:S(2)}) async-start(), calls=%async_computation.3 | async-start | bytes 11141120 | tf_op jit(solution)/shard_map/all_gather | solution.py:30
  118.0 239.3 %reduce-scatter.5.cloned.1.call-start = ((), (), s32[]{:S(2)}) async-start(), calls=%async_computation.4 | async-start | bytes 14745600 | tf_op jit(solution)/shard_map/reduce_scatter | solution.py:34
Sparse Core Ops, SparseCore 0:
  32.7 80.9 reduce-scatter.2
  118.1 60.7 all-gather.1
  200.7 156.5 reduce-scatter.4
where the time goes:
time: 364 us
  waiting for transfers between devices  297 us (82%)
  matrix products  46.9 us (13%)
  between operations  13.8 us (4%)
  other arithmetic  4.85 us (1%)
    reduce_scatter x1, waiting for transfers between devices, local(): lax.psum_scatter(partial_value.astype(jnp.bfloat16), 'dp', scatter_dimens...  157 us
    reduce_scatter x1, waiting for transfers between devices, local(): lax.psum_scatter(lax.dot_general(grad_pre, w_in, (((1,), (1,)), ((), ()))...  79.5 us
    all_gather x1, waiting for transfers between devices, local(): normed_all = lax.all_gather(outgoing, 'tensor', axis=0, tiled=True)  60.7 us
    dot_general x1, matrix products, local(): lax.dot_general(grad_pre, w_in, (((1,), (1,)), ((), ())), preferred_eleme...  25.3 us
    dot_general x1, matrix products, local(): lax.dot_general(normed_all, grad_pre, (((0,), (0,)), ((), ())), preferred...  21.6 us
  transfers between devices with their start and end apart: 3, of which 3 were waited for; matrix products, arithmetic and copies ran while one was open for 0% of the time, Pallas kernels for 0%

commit v1 on v0

v1 whole, which is shorter than its diff:
```python
import functools

import jax
import jax.numpy as jnp
from jax import lax
from jax.experimental import pallas as pl
from jax.experimental.pallas import tpu as pltpu
from jax.sharding import PartitionSpec as P

AXES = ("dp", "tensor")
CHUNKS = ((512, 768), (0, 512))
BF16 = jnp.bfloat16
F32 = jnp.float32
FEW = pltpu.CompilerParams(vmem_limit_bytes=16 << 20)
ROOM = pltpu.CompilerParams(vmem_limit_bytes=58 << 20)


def lasting(microseconds):
    return pl.CostEstimate(flops=int(microseconds * 0.55e9), bytes_accessed=1 << 16, transcendentals=0)


def moved(value, z=0, x=0, y=0, y_lo=0, core=0):
    pairs = []
    for source in range(128):
        yh, zz, yl, xx, cc = source // 64, source // 16 % 4, source // 8 % 2, source // 2 % 4, source % 2
        row = (yh * 2 + (yl ^ y_lo) + y) % 4
        target = ((row // 2 * 4 + (zz + z) % 4) * 2 + row % 2) * 8 + (xx + x) % 4 * 2 + (cc ^ core)
        pairs.append((source, target))
    return lax.ppermute(value, AXES, pairs)


def after(value, *others):
    return lax.optimization_barrier((value, *others))[0]


def like(*shape, kind=BF16):
    return jax.ShapeDtypeStruct(shape, kind)


def wide(ref):
    return ref[...].astype(F32)


def small(kernel, outs, *values, scratch=()):
    return pl.pallas_call(
        kernel,
        grid=(1,),
        in_specs=[pl.BlockSpec(value.shape, lambda i: (0, 0)) for value in values],
        out_specs=[pl.BlockSpec(out.shape, lambda i: (0, 0)) for out in outs],
        out_shape=outs,
        scratch_shapes=scratch,
        compiler_params=FEW,
        cost_estimate=lasting(1.2),
    )(*values)


def unit(values):
    center = jnp.mean(values, axis=1, keepdims=True)
    shifted = values - center
    inv_std = lax.rsqrt(jnp.mean(shifted * shifted, axis=1, keepdims=True) + 1e-05)
    return shifted * inv_std, inv_std


def normed_kernel(starts, rows_ref, gain_ref, *refs):
    *outs, normed = refs
    normed[...] = unit(wide(rows_ref))[0] * gain_ref[...]
    for i in range(8):
        begin = pl.multiple_of(starts[i], 128)
        outs[i // 2][:, i % 2 * 640 : i % 2 * 640 + 640] = normed[:, pl.ds(begin, 640)].astype(BF16)


def normed_blocks(starts, rows, gain):
    return pl.pallas_call(
        normed_kernel,
        grid_spec=pltpu.PrefetchScalarGridSpec(
            num_scalar_prefetch=1,
            grid=(1,),
            in_specs=[pl.BlockSpec((64, 5120), lambda i, s: (0, 0)), pl.BlockSpec((1, 5120), lambda i, s: (0, 0))],
            out_specs=[pl.BlockSpec((64, 1280), lambda i, s: (0, 0))] * 4,
            scratch_shapes=[pltpu.VMEM((64, 5120), F32)],
        ),
        out_shape=[like(64, 1280)] * 4,
        compiler_params=FEW,
        cost_estimate=lasting(1.2),
    )(starts, rows, gain)


def turn_kernel(*refs):
    rows = jnp.concatenate([wide(ref) for ref in refs[:4]], axis=0)
    refs[4][...] = rows.T.astype(BF16)


def turned(parts):
    return small(turn_kernel, [like(1280, 256)], *parts)[0]


def slope_kernel(places, pre_ref, hidden_ref, *outs):
    step = pl.program_id(0)
    for row in range(0, 256, 32):
        rows = pl.ds(row, 32)
        place = pl.multiple_of(places[4 * step + row // 64] * 64 + row % 64, 32)
        for begin in range(0, 1280, 256):
            v = pre_ref[rows, begin : begin + 256].astype(F32)
            square = v * v
            s = 1.0 / (1.0 + jnp.exp(v * (-2.0 * 0.7978845608 - (2.0 * 0.7978845608 * 0.044715) * square)))
            rate = v * (2.0 * 0.7978845608 + (6.0 * 0.7978845608 * 0.044715) * square)
            hidden = hidden_ref[rows, begin : begin + 256].astype(F32)
            grad_pre = (hidden * (s + s * (rate - rate * s))).astype(BF16)
            outs[-1][pl.ds(place, 32), begin : begin + 256] = grad_pre
            for out, (first, width) in zip(outs, CHUNKS):
                if first <= begin < first + width:
                    out[(begin - first) // 256, rows, :] = grad_pre


def grad_pre_of(places, pre_gelu, grad_hidden):
    block = pl.BlockSpec((256, 1280), lambda i, places: (i, 0))
    return pl.pallas_call(
        slope_kernel,
        grid_spec=pltpu.PrefetchScalarGridSpec(
            num_scalar_prefetch=1,
            grid=(4,),
            in_specs=[block, block],
            out_specs=[pl.BlockSpec((width // 256, 256, 256), lambda i, places: (0, i, 0)) for _, width in CHUNKS]
            + [pl.BlockSpec((1024, 1280), lambda i, places: (0, 0))],
        ),
        out_shape=[like(width // 256, 1024, 256) for _, width in CHUNKS] + [like(1024, 1280)],
        compiler_params=ROOM,
        cost_estimate=lasting(5),
    )(places, pre_gelu, grad_hidden)


def back_kernel(rows_ref, w_ref, own_ref, *far_refs):
    product = lax.dot_general(rows_ref[...], w_ref[...], (((1,), (1,)), ((), ())), preferred_element_type=F32)
    own_ref[...] = product[:512].astype(BF16)
    far_refs[0][...] = product[512:768].astype(BF16)
    far_refs[1][...] = product[768:].astype(BF16)


def back(rows, w_in, side):
    counts = (512, 256, 256)
    return pl.pallas_call(
        back_kernel,
        grid=(5,),
        in_specs=[
            pl.BlockSpec((1024, 1280), lambda i: (0, 0)),
            pl.BlockSpec((512, 1280), lambda i: (5 * side + i, 0)),
        ],
        out_specs=[pl.BlockSpec((count, 512), lambda i: (0, i)) for count in counts],
        out_shape=[like(count, 2560) for count in counts],
        compiler_params=ROOM,
        cost_estimate=lasting(1),
    )(rows, w_in)


def add_left_kernel(own_ref, *refs):
    for i in range(2):
        refs[2 + i][...] = (wide(own_ref.at[pl.ds(256 * i, 256)]) + wide(refs[i])).astype(BF16)


def add_right_kernel(own_ref, near_ref, core_ref, front_ref, rear_ref, next_ref, last_ref, keep_ref):
    def block(i, begin):
        core = (near_ref, core_ref)[i].at[pl.ds(begin, 64)]
        return (wide(own_ref.at[pl.ds(256 * i + begin, 64)]) + wide(core)).astype(BF16)

    front_ref[...] = block(0, 128)
    rear_ref[...] = block(1, 128)
    for ref, begin in ((next_ref, 64), (last_ref, 192), (keep_ref, 0)):
        ref[:64] = block(0, begin)
        ref[64:] = block(1, begin)


def added(kernel, counts, own, far):
    return pl.pallas_call(
        kernel,
        grid=(2,),
        in_specs=[pl.BlockSpec((count, 1280), lambda i: (0, i)) for count in (512, 256, 256)],
        out_specs=[pl.BlockSpec((count, 1280), lambda i: (0, i)) for count in counts],
        out_shape=[like(count, 2560) for count in counts],
        compiler_params=FEW,
        cost_estimate=lasting(1),
    )(own, *[moved(half, core=1) for half in far])


def split_left_kernel(keep_ref, other_ref, front_ref, rear_ref, next_ref, last_ref, own_ref):
    total = (wide(keep_ref) + wide(other_ref)).astype(BF16)
    own_ref[...] = total[:64]
    next_ref[...] = total[64:128]
    front_ref[...] = total[128:160]
    rear_ref[...] = total[160:192]
    last_ref[...] = total[192:]


def join_kernel(next_ref, last_ref, front_ref, rear_ref, ahead_ref, behind_ref):
    half = next_ref.shape[0] // 2
    ahead_ref[:half] = (wide(next_ref.at[:half]) + wide(front_ref)).astype(BF16)
    ahead_ref[half:] = next_ref[half:]
    behind_ref[:half] = last_ref[:half]
    behind_ref[half:] = (wide(last_ref.at[half:]) + wide(rear_ref)).astype(BF16)


def right_sum_kernel(own_ref, ahead_ref, behind_ref, keep_ref, send_ref):
    total = wide(own_ref) + wide(ahead_ref) + wide(behind_ref)
    keep_ref[...] = total[:64]
    send_ref[...] = total[64:].astype(BF16)


def end_kernel(rows_ref, gain_ref, out_grad_ref, own_ref, ahead_ref, behind_ref, keep_ref, send_ref, grad_ref, scaled):
    scaled[:, :2560] = wide(own_ref) + wide(ahead_ref) + wide(behind_ref)
    scaled[:, 2560:] = keep_ref[...] + wide(send_ref)
    unit_rows, inv_std = unit(wide(rows_ref))
    value = scaled[...] * gain_ref[...]
    mean = jnp.mean(value, axis=1, keepdims=True)
    slant = jnp.mean(value * unit_rows, axis=1, keepdims=True)
    grad_ref[...] = (wide(out_grad_ref) + inv_std * (value - mean - unit_rows * slant)).astype(BF16)


def add_halves(out_ref, value, up_ref, down_ref):
    out_ref[:320] = (value[:320].astype(F32) + up_ref[0].astype(F32)).astype(BF16)
    out_ref[320:] = (value[320:].astype(F32) + down_ref[0].astype(F32)).astype(BF16)


def weight_kernel(task, columns_ref, *refs):
    pieces, refs = refs[:4], refs[4:]
    total = None
    for begin in range(0, 16, 4):
        blocks = range(begin, begin + 4)
        left = jnp.concatenate([columns_ref[b] for b in blocks], axis=1)
        right = jnp.concatenate([piece[0, b * 64 : b * 64 + 64, :] for b in blocks for piece in pieces], axis=0)
        term = jnp.dot(left, right, preferred_element_type=F32)
        total = term if total is None else total + term
    if task == "send":
        refs[0][0] = total[:320].astype(BF16)
        refs[1][0] = total[320:].astype(BF16)
    elif task == "keep":
        refs[0][0] = total.astype(BF16)
    else:
        add_halves(refs[2], total, refs[0], refs[1])


def weight(task, columns, pieces, other=()):
    steps = pieces[0].shape[0]
    half = pl.BlockSpec((1, 320, 256), lambda i: (i, 0, 0))
    if task == "send":
        outs, shapes = [half, half], [like(steps, 320, 256)] * 2
    elif task == "keep":
        outs, shapes = [pl.BlockSpec((1, 640, 256), lambda i: (i, 0, 0))], [like(steps, 640, 256)]
    else:
        outs, shapes = [pl.BlockSpec((640, 256), lambda i: (0, 2 + i))], [like(640, 1280)]
    return pl.pallas_call(
        functools.partial(weight_kernel, task),
        grid=(steps,),
        in_specs=[pl.BlockSpec((16, 640, 256), lambda i: (0, int(task == "send"), 0))]
        + [pl.BlockSpec((1, 1024, 256), lambda i: (i, 0, 0))] * 4
        + [half] * len(other),
        out_specs=outs,
        out_shape=shapes,
        compiler_params=ROOM,
        cost_estimate=lasting(1.5 + 1.8 * steps),
    )(columns, *pieces, *other)


def put_kernel(keep_ref, up_ref, down_ref, given_ref, out_ref):
    add_halves(out_ref, keep_ref[0], up_ref, down_ref)


def put(keep, up, down, given):
    half = pl.BlockSpec((1, 320, 256), lambda i: (i, 0, 0))
    return pl.pallas_call(
        put_kernel,
        grid=(2,),
        in_specs=[pl.BlockSpec((1, 640, 256), lambda i: (i, 0, 0)), half, half, pl.BlockSpec(memory_space=pl.ANY)],
        out_specs=pl.BlockSpec((640, 256), lambda i: (0, i)),
        out_shape=like(640, 1280),
        input_output_aliases={3: 0},
        compiler_params=ROOM,
        cost_estimate=lasting(2),
    )(keep, up, down, given)


def local(inputs, norm_gain, w_in, pre_gelu, grad_hidden, grad_out):
    group, place = lax.axis_index("dp"), lax.axis_index("tensor")
    y_hi, z = group // 4, group % 4
    y_lo, x, core = place // 8, place // 2 % 4, place % 2
    gain = norm_gain.reshape(1, 5120)

    step = jnp.arange(8, dtype=jnp.int32)
    starts = (((y_hi ^ (step % 2)) * 4 + (z + step // 2) % 4) * 640).astype(jnp.int32)
    block = jnp.arange(16, dtype=jnp.int32)
    places = ((core ^ (block % 2)) * 8 + (y_lo ^ (block // 8)) * 4 + (block // 2 % 4 - x + 4) % 4).astype(jnp.int32)

    blocks = normed_blocks(starts, inputs, gain)
    parts = [blocks[0], moved(blocks[3], z=-1), moved(blocks[2], z=2), moved(blocks[1], z=1)]
    *chunks, rows = grad_pre_of(after(places, *blocks), pre_gelu, grad_hidden)
    one = turned([after(parts[0], rows), *parts[1:]])
    columns = lax.all_gather(one, "tensor", axis=0, tiled=False)

    first = [moved(chunks[0], z=-1), moved(chunks[0], z=1)]

    own_right, *far_right = back(after(rows, one), w_in, 1)
    own_left, *far_left = back(after(rows, own_right), w_in, 0)
    own_right = after(own_right, own_left, *first)
    front, rear, next_right, last_right, own_right = added(
        add_right_kernel, [64, 64, 128, 128, 128], own_right, far_right
    )
    front, rear = moved(front, x=1), moved(rear, x=-1)
    keep, send = added(add_left_kernel, [256, 256], after(own_left, own_right), far_left)
    send = moved(send, y_lo=1)

    first_far = moved(first[1], z=1)
    second_next = moved(after(chunks[1], *first), z=-1)
    ahead, behind = small(join_kernel, [like(128, 2560)] * 2, next_right, last_right, front, rear)
    second_far = moved(after(second_next, ahead), z=-1)
    second_last = moved(after(chunks[1], second_next, ahead), z=1)
    pieces = [[chunks[0], first[0], first_far, first[1]], [chunks[1], second_next, second_far, second_last]]
    ahead, behind = moved(ahead, x=1), moved(behind, x=-1)

    sent = weight("send", after(columns, second_next, ahead, behind), pieces[0])
    hop = [moved(sent[0], y=1), moved(sent[1], y=-1)]
    other = [moved(hop[0], y=1), moved(hop[1], y=-1)]

    right_keep, right_send = small(
        right_sum_kernel, [like(64, 2560, kind=F32), like(64, 2560)], after(own_right, *sent), ahead, behind
    )
    right_send = moved(right_send, y_lo=1)
    outs = [like(count, 2560) for count in (32, 32, 64, 64, 64)]
    keep = after(keep, *sent)
    front, rear, next_left, last_left, own_left = small(split_left_kernel, outs, keep, send)
    front, rear = moved(front, x=1), moved(rear, x=-1)
    sides = small(join_kernel, [like(64, 2560)] * 2, next_left, last_left, front, rear)
    ahead, behind = moved(sides[0], x=1), moved(sides[1], x=-1)

    sent = weight("send", after(columns, right_keep, *sides, *hop), pieces[1])
    hop = [moved(sent[0], y=1), moved(sent[1], y=-1)]
    (kept,) = weight("keep", after(columns, *sent), pieces[1])
    (grad_w_in,) = weight("put", after(columns, kept), pieces[0], other)
    (grad_in,) = small(
        end_kernel,
        [like(64, 5120)],
        inputs,
        gain,
        grad_out,
        after(own_left, grad_w_in),
        ahead,
        behind,
        right_keep,
        right_send,
        scratch=[pltpu.VMEM((64, 5120), F32)],
    )
    grad_w_in = put(after(kept, grad_in), moved(hop[0], y=1), moved(hop[1], y=-1), grad_w_in)
    return (grad_in, grad_w_in)


def solution(mesh):
    placed = (
        P(("dp", "tensor"), None),
        P(),
        P(None, "tensor"),
        P("dp", "tensor"),
        P("dp", "tensor"),
        P(("dp", "tensor"), None),
    )
    return jax.shard_map(
        local,
        mesh=mesh,
        in_specs=placed,
        out_specs=(P(("dp", "tensor"), None), P("dp", "tensor")),
        check_vma=False,
    )
```

time: 364 us -> 183 us (0.50)
  waiting for transfers between devices: 297 us -> 46.4 us
  Pallas kernels: 0 us -> 71.5 us
  matrix products: 46.9 us -> 0 us
  starting transfers between devices: 0.3 us -> 44.8 us
  other arithmetic: 4.85 us -> 0.54 us
  local copies, waits for them, and re-layouts: 1.01 us -> 4.97 us
    reduce_scatter x2 -> x0, waiting for transfers between devices: 236 us -> none  [the longest x1 157 us: local(): lax.psum_scatter(partial_value.astype(jnp.bfloat16), 'dp', scatter_dimens...]
    pallas_call x0 -> x17, Pallas kernels: none -> 71.5 us  [the longest x4 31.1 us: weight(): pl.pallas_call(functools.partial(weight_kernel, task), grid=(steps,), in_...]
    all_gather x1, waiting for transfers between devices: 60.7 us -> 0.01 us  [local(): columns = lax.all_gather(one, 'tensor', axis=0, tiled=False)]
    dot_general x2 -> x0, matrix products: 46.9 us -> none  [the longest x1 25.3 us: local(): lax.dot_general(grad_pre, w_in, (((1,), (1,)), ((), ())), preferred_eleme...]
    ppermute x0 -> x31, waiting for transfers between devices: none -> 46.4 us  [moved(): return lax.ppermute(value, AXES, pairs)]
    ppermute x0 -> x31, starting transfers between devices: none -> 44.7 us  [moved(): return lax.ppermute(value, AXES, pairs)]
    unnamed x6 -> x30, local copies, waits for them, and re-layouts: 1.01 us -> 4.97 us
  transfers between devices with their start and end apart: 3 -> 32, of which waited for: 3 -> 9; matrix products, arithmetic and copies ran while one was open for 0% -> 0% of each run, Pallas kernels for 0% -> 37%
where the time goes in v1:
time: 183 us; the launch traced here: 182 us
  Pallas kernels  71.5 us (39%)
  waiting for transfers between devices  46.4 us (25%)
  starting transfers between devices  44.8 us (24%)
  between operations  14.2 us (8%)
  local copies, waits for them, and re-layouts  4.97 us (3%)
    ppermute x31, waiting for transfers between devices, moved(): return lax.ppermute(value, AXES, pairs)  46.4 us
    ppermute x31, starting transfers between devices, moved(): return lax.ppermute(value, AXES, pairs)  44.7 us
    pallas_call x4, Pallas kernels, weight(): pl.pallas_call(functools.partial(weight_kernel, task), grid=(steps,), in_...  31.1 us
    pallas_call x2, Pallas kernels, back(): pl.pallas_call(back_kernel, grid=(5,), in_specs=[pl.BlockSpec((1024, 1280...  22.1 us
    pallas_call x1, Pallas kernels, grad_pre_of(): pl.pallas_call(slope_kernel, grid_spec=pltpu.PrefetchScalarGridSpec(num_s...  7.92 us
    unnamed x30, local copies, waits for them, and re-layouts  4.97 us
    pallas_call x6, Pallas kernels, small(): pl.pallas_call(kernel, grid=(1,), in_specs=[pl.BlockSpec(value.shape, lam...  4.01 us
  transfers between devices with their start and end apart: 32, of which 9 were waited for; matrix products, arithmetic and copies ran while one was open for 0% of the time, Pallas kernels for 37%

profile of v1, /device:TPU:0, one launch (start us, length us, event | category | flops | bytes accessed | tf_op | source)
XLA Modules:
  0.0 182.4 jit_solution(11361757214300452407)
XLA Ops:
  10.2 4.2 %collective-permute-start = (bf16[64,1280]{1,0:T(8,128)(2,1)S(1)}, bf16[64,1280]{1,0:T(8,128)(2,1)S(1)}, u32[]{:S(2)}, u32[]{:S(2)}) collective-permute-start(bf16[64,1280]{1,0:T(8,128)(2,1)S(1)} %get-tuple-element.57), channel_id=1, source_target_pairs={{0,48},{1,49},{2,50},{3,51},{4,52},{5,53},{6,54},{7,55},{8,56},{9,... | collective-permute-start | bytes 491528 | tf_op jit(solution)/shard_map/ppermute | solution.py:29
  16.2 7.9 %shard_map.78 = (bf16[3,1024,256]{2,1,0:T(8,128)(2,1)}, bf16[2,1024,256]{2,1,0:T(8,128)(2,1)}, bf16[1024,1280]{1,0:T(8,128)(2,1)}) custom-call(s32[16]{0:T(128)} %fusion.places, bf16[1024,1280]{1,0:T(8,128)(2,1)} %pre_ref.1, bf16[1024,1280]{1,0:T(8,128)(2,1)} %hidden_ref.1), custom_call_target="tpu_custom_call" | custom-call | flops 2750000128 | bytes 65536 | tf_op jit(solution)/shard_map/pallas_call | solution.py:117
  28.0 11.0 %shard_map.80 = (bf16[512,2560]{1,0:T(8,128)(2,1)}, bf16[256,2560]{1,0:T(8,128)(2,1)}, bf16[256,2560]{1,0:T(8,128)(2,1)}) custom-call(bf16[1024,1280]{1,0:T(8,128)(2,1)} %get-tuple-element.63.rows_ref, bf16[5120,1280]{1,0:T(8,128)(2,1)} %w_ref.3), custom_call_target="tpu_custom_call" | custom-call | flops 550000000 | bytes 65536 | tf_op jit(solution)/shard_map/pallas_call | solution.py:141
  39.5 11.1 %shard_map.81 = (bf16[512,2560]{1,0:T(8,128)(2,1)}, bf16[256,2560]{1,0:T(8,128)(2,1)}, bf16[256,2560]{1,0:T(8,128)(2,1)}) custom-call(bf16[1024,1280]{1,0:T(8,128)(2,1)} %get-tuple-element.63.rows_ref, bf16[5120,1280]{1,0:T(8,128)(2,1)} %w_ref.3), custom_call_target="tpu_custom_call" | custom-call | flops 550000000 | bytes 65536 | tf_op jit(solution)/shard_map/pallas_call | solution.py:141
  50.6 11.6 %collective-permute-done.3.refs_1_ = bf16[3,1024,256]{2,1,0:T(8,128)(2,1)} collective-permute-done((bf16[3,1024,256]{2,1,0:T(8,128)(2,1)}, bf16[3,1024,256]{2,1,0:T(8,128)(2,1)}, u32[]{:S(2)}, u32[]{:S(2)}) %collective-permute-start.3) | collective-permute-done | bytes 1572896 | tf_op jit(solution)/shard_map/ppermute | solution.py:29
  64.1 3.2 %collective-permute-start.9 = (bf16[2,1024,256]{2,1,0:T(8,128)(2,1)}, bf16[2,1024,256]{2,1,0:T(8,128)(2,1)}, u32[]{:S(2)}, u32[]{:S(2)}) collective-permute-start(bf16[2,1024,256]{2,1,0:T(8,128)(2,1)} %get-tuple-element.98.refs_0_), channel_id=1, source_target_pairs={{0,48},{1,49},{2,50},{3,51},{4,52},{5,53},{6,54},{7,55},{8,56},{9,... | collective-permute-start | bytes 3145736 | tf_op jit(solution)/shard_map/ppermute | solution.py:29
  71.9 1.9 %shard_map.83 = (bf16[256,2560]{1,0:T(8,128)(2,1)S(1)}, bf16[256,2560]{1,0:T(8,128)(2,1)}) custom-call(bf16[512,2560]{1,0:T(8,128)(2,1)S(1)} %copy-done, bf16[256,2560]{1,0:T(8,128)(2,1)S(1)} %collective-permute-done.7.refs_0_, bf16[256,2560]{1,0:T(8,128)(2,1)S(1)} %collective-permute-done.8.refs_1_), custom_call_target="tpu_custom_call" | custom-call | flops 550000000 | bytes 65536 | tf_op jit(solution)/shard_map/pallas_call | solution.py:173
  75.3 8.9 %collective-permute-done.10.front_ref = bf16[64,2560]{1,0:T(8,128)(2,1)S(1)} collective-permute-done((bf16[64,2560]{1,0:T(8,128)(2,1)S(1)}, bf16[64,2560]{1,0:T(8,128)(2,1)S(1)}, u32[]{:S(2)}, u32[]{:S(2)}) %collective-permute-start.10) | collective-permute-done | bytes 327712 | tf_op jit(solution)/shard_map/ppermute | solution.py:29
  84.2 2.4 %collective-permute-done.11.rear_ref = bf16[64,2560]{1,0:T(8,128)(2,1)S(1)} collective-permute-done((bf16[64,2560]{1,0:T(8,128)(2,1)S(1)}, bf16[64,2560]{1,0:T(8,128)(2,1)S(1)}, u32[]{:S(2)}, u32[]{:S(2)}) %collective-permute-start.11) | collective-permute-done | bytes 327712 | tf_op jit(solution)/shard_map/ppermute | solution.py:29
  90.1 2.2 %collective-permute-start.20 = (bf16[2,1024,256]{2,1,0:T(8,128)(2,1)}, bf16[2,1024,256]{2,1,0:T(8,128)(2,1)}, u32[]{:S(2)}, u32[]{:S(2)}) collective-permute-start(bf16[2,1024,256]{2,1,0:T(8,128)(2,1)} %collective-permute-done.9.refs_1_), channel_id=1, source_target_pairs={{0,48},{1,49},{2,50},{3,51},{4,52},{5,53},{6,54},{7,55},{8,56},{9,... | collective-permute-start | bytes 3145736 | tf_op jit(solution)/shard_map/ppermute | solution.py:29
  92.3 12.8 %collective-permute-done.12.ahead_ref = bf16[128,2560]{1,0:T(8,128)(2,1)S(1)} collective-permute-done((bf16[128,2560]{1,0:T(8,128)(2,1)S(1)}, bf16[128,2560]{1,0:T(8,128)(2,1)S(1)}, u32[]{:S(2)}, u32[]{:S(2)}) %collective-permute-start.12) | collective-permute-done | bytes 655392 | tf_op jit(solution)/shard_map/ppermute | solution.py:29
  108.6 8.5 %shard_map.85 = (bf16[3,320,256]{2,1,0:T(8,128)(2,1)}, bf16[3,320,256]{2,1,0:T(8,128)(2,1)}) custom-call(bf16[16,1280,256]{2,1,0:T(8,128)(2,1)} %bitcast.4, bf16[3,1024,256]{2,1,0:T(8,128)(2,1)} %get-tuple-element.65.refs_0_, bf16[3,1024,256]{2,1,0:T(8,128)(2,1)} %collective-permute-done.3.refs_1_, bf16[3,1024,256]{2,1,0:T(8,128)(2,1)} %collective-permute-done.14.refs_2_, ...), custom_call_target="tpu_custom_call" | custom-call | flops 3795000064 | bytes 65536 | tf_op jit(solution)/shard_map/pallas_call | solution.py:249
  120.7 2.6 %collective-permute-start.16 = (bf16[32,2560]{1,0:T(8,128)(2,1)S(1)}, bf16[32,2560]{1,0:T(8,128)(2,1)S(1)}, u32[]{:S(2)}, u32[]{:S(2)}) collective-permute-start(bf16[32,2560]{1,0:T(8,128)(2,1)S(1)} %get-tuple-element.92), channel_id=1, source_target_pairs={{0,2},{1,3},{2,4},{3,5},{4,6},{5,7},{6,0},{7,1},{8,10},{9,11},{10,... | collective-permute-start | bytes 491528 | tf_op jit(solution)/shard_map/ppermute | solution.py:29
  123.2 4.8 %collective-permute-done.16.front_ref = bf16[32,2560]{1,0:T(8,128)(2,1)S(1)} collective-permute-done((bf16[32,2560]{1,0:T(8,128)(2,1)S(1)}, bf16[32,2560]{1,0:T(8,128)(2,1)S(1)}, u32[]{:S(2)}, u32[]{:S(2)}) %collective-permute-start.16) | collective-permute-done | bytes 163872 | tf_op jit(solution)/shard_map/ppermute | solution.py:29
  128.0 2.0 %collective-permute-start.17 = (bf16[32,2560]{1,0:T(8,128)(2,1)S(1)}, bf16[32,2560]{1,0:T(8,128)(2,1)S(1)}, u32[]{:S(2)}, u32[]{:S(2)}) collective-permute-start(bf16[32,2560]{1,0:T(8,128)(2,1)S(1)} %get-tuple-element.93), channel_id=1, source_target_pairs={{0,6},{1,7},{2,0},{3,1},{4,2},{5,3},{6,4},{7,5},{8,14},{9,15},{10,... | collective-permute-start | bytes 491528 | tf_op jit(solution)/shard_map/ppermute | solution.py:29
  130.3 3.1 %collective-permute-done.17.rear_ref = bf16[32,2560]{1,0:T(8,128)(2,1)S(1)} collective-permute-done((bf16[32,2560]{1,0:T(8,128)(2,1)S(1)}, bf16[32,2560]{1,0:T(8,128)(2,1)S(1)}, u32[]{:S(2)}, u32[]{:S(2)}) %collective-permute-start.17) | collective-permute-done | bytes 163872 | tf_op jit(solution)/shard_map/ppermute | solution.py:29
  133.8 3.0 %collective-permute-start.23 = (bf16[3,320,256]{2,1,0:T(8,128)(2,1)}, bf16[3,320,256]{2,1,0:T(8,128)(2,1)S(1)}, u32[]{:S(2)}, u32[]{:S(2)}) collective-permute-start(bf16[3,320,256]{2,1,0:T(8,128)(2,1)} %collective-permute-done.19), channel_id=1, source_target_pairs={{0,72},{1,73},{2,74},{3,75},{4,76},{5,77},{6,78},{7,79},{8,0},{9,1... | collective-permute-start | bytes 1474568 | tf_op jit(solution)/shard_map/ppermute | solution.py:29
  136.8 6.9 %shard_map.89 = (bf16[2,320,256]{2,1,0:T(8,128)(2,1)}, bf16[2,320,256]{2,1,0:T(8,128)(2,1)}) custom-call(bf16[16,1280,256]{2,1,0:T(8,128)(2,1)} %bitcast.5, bf16[2,1024,256]{2,1,0:T(8,128)(2,1)} %get-tuple-element.98.refs_0_, bf16[2,1024,256]{2,1,0:T(8,128)(2,1)} %collective-permute-done.9.refs_1_, bf16[2,1024,256]{2,1,0:T(8,128)(2,1)} %collective-permute-done.20.refs_2_, ...), custom_call_target="tpu_custom_call" | custom-call | flops 2804999936 | bytes 65536 | tf_op jit(solution)/shard_map/pallas_call | solution.py:249
  143.7 3.2 %collective-permute-start.29 = (bf16[2,320,256]{2,1,0:T(8,128)(2,1)}, bf16[2,320,256]{2,1,0:T(8,128)(2,1)}, u32[]{:S(2)}, u32[]{:S(2)}) collective-permute-start(bf16[2,320,256]{2,1,0:T(8,128)(2,1)} %get-tuple-element.100), channel_id=1, source_target_pairs={{0,72},{1,73},{2,74},{3,75},{4,76},{5,77},{6,78},{7,79},{8,0},{9,1... | collective-permute-start | bytes 983048 | tf_op jit(solution)/shard_map/ppermute | solution.py:29
  146.9 7.0 %shard_map.90.keep_ref = bf16[2,640,256]{2,1,0:T(8,128)(2,1)} custom-call(bf16[16,1280,256]{2,1,0:T(8,128)(2,1)} %bitcast.6, bf16[2,1024,256]{2,1,0:T(8,128)(2,1)} %get-tuple-element.98.refs_0_, bf16[2,1024,256]{2,1,0:T(8,128)(2,1)} %collective-permute-done.9.refs_1_, bf16[2,1024,256]{2,1,0:T(8,128)(2,1)} %collective-permute-done.20.refs_2_, ...), custom_call_target="tpu_custom_call" | custom-call | flops 2804999936 | bytes 65536 | tf_op jit(solution)/shard_map/pallas_call | solution.py:249
  154.7 3.0 %collective-permute-start.25 = (bf16[64,2560]{1,0:T(8,128)(2,1)S(1)}, bf16[64,2560]{1,0:T(8,128)(2,1)S(1)}, u32[]{:S(2)}, u32[]{:S(2)}) collective-permute-start(bf16[64,2560]{1,0:T(8,128)(2,1)S(1)} %get-tuple-element.95), channel_id=1, source_target_pairs={{0,6},{1,7},{2,0},{3,1},{4,2},{5,3},{6,4},{7,5},{8,14},{9,15},{10,... | collective-permute-start | bytes 983048 | tf_op jit(solution)/shard_map/ppermute | solution.py:29
  161.0 8.8 %shard_map.91.given_ref = bf16[640,1280]{1,0:T(8,128)(2,1)} custom-call(bf16[16,1280,256]{2,1,0:T(8,128)(2,1)} %bitcast.7, bf16[3,1024,256]{2,1,0:T(8,128)(2,1)} %get-tuple-element.65.refs_0_, bf16[3,1024,256]{2,1,0:T(8,128)(2,1)} %collective-permute-done.3.refs_1_, bf16[3,1024,256]{2,1,0:T(8,128)(2,1)} %collective-permute-done.14.refs_2_, ...), custom_call_target="tpu_custom_call" | custom-call | flops 3795000064 | bytes 65536 | tf_op jit(solution)/shard_map/pallas_call | solution.py:249
  169.8 2.1 %shard_map.92 = bf16[64,5120]{1,0:T(8,128)(2,1)} custom-call(bf16[64,5120]{1,0:T(8,128)(2,1)S(1)} %copy-done.3, f32[1,5120]{1,0:T(1,128)S(1)} %bitcast.3, bf16[64,5120]{1,0:T(8,128)(2,1)S(1)} %copy-done.4, bf16[64,2560]{1,0:T(8,128)(2,1)S(1)} %get-tuple-element.103.own_ref, bf16[64,2560]{1,0:T(8,128)(2,1)S(1)} %collective-permute-done.24.ahead_ref, ...), custom_call_target="tpu_custom_call" | custom-call | flops 660000000 | bytes 65536 | tf_op jit(solution)/shard_map/pallas_call | solution.py:45
  173.5 2.1 %shard_map.93 = bf16[640,1280]{1,0:T(8,128)(2,1)} custom-call(bf16[2,640,256]{2,1,0:T(8,128)(2,1)} %shard_map.90.keep_ref, bf16[2,320,256]{2,1,0:T(8,128)(2,1)} %copy-done.13, bf16[2,320,256]{2,1,0:T(8,128)(2,1)} %copy-done.14, bf16[640,1280]{1,0:T(8,128)(2,1)} %shard_map.91.given_ref), custom_call_target="tpu_custom_call", output_to_operand_aliasing={{}: (3, {})} | custom-call | flops 1100000000 | bytes 65536 | tf_op jit(solution)/shard_map/pallas_call | solution.py:268
  (90 shorter events, 33.9 us)
Async XLA Ops:
  7.2 101.4 %all-gather.3.cloned.1.call-start = ((), (), s32[]{:S(2)}) async-start(), calls=%async_computation | async-start | bytes 11141120 | tf_op jit(solution)/shard_map/all_gather | solution.py:295
  10.2 13.9 %collective-permute-start = (bf16[64,1280]{1,0:T(8,128)(2,1)S(1)}, bf16[64,1280]{1,0:T(8,128)(2,1)S(1)}, u32[]{:S(2)}, u32[]{:S(2)}) collective-permute-start(bf16[64,1280]{1,0:T(8,128)(2,1)S(1)} %get-tuple-element.57), channel_id=1, source_target_pairs={{0,48},{1,49},{2,50},{3,51},{4,52},{5,53},{6,54},{7,55},{8,56},{9,... | collective-permute-start | bytes 491528 | tf_op jit(solution)/shard_map/ppermute | solution.py:29
  25.9 36.4 %collective-permute-start.3 = (bf16[3,1024,256]{2,1,0:T(8,128)(2,1)}, bf16[3,1024,256]{2,1,0:T(8,128)(2,1)}, u32[]{:S(2)}, u32[]{:S(2)}) collective-permute-start(bf16[3,1024,256]{2,1,0:T(8,128)(2,1)} %get-tuple-element.65.refs_0_), channel_id=1, source_target_pairs={{0,48},{1,49},{2,50},{3,51},{4,52},{5,53},{6,54},{7,55},{8,56},{9,... | collective-permute-start | bytes 4718600 | tf_op jit(solution)/shard_map/ppermute | solution.py:29
  27.3 36.8 %collective-permute-start.4 = (bf16[3,1024,256]{2,1,0:T(8,128)(2,1)}, bf16[3,1024,256]{2,1,0:T(8,128)(2,1)}, u32[]{:S(2)}, u32[]{:S(2)}) collective-permute-start(bf16[3,1024,256]{2,1,0:T(8,128)(2,1)} %get-tuple-element.65.refs_0_), channel_id=1, source_target_pairs={{0,16},{1,17},{2,18},{3,19},{4,20},{5,21},{6,22},{7,23},{8,24},{9,... | collective-permute-start | bytes 4718600 | tf_op jit(solution)/shard_map/ppermute | solution.py:29
  39.0 25.1 %collective-permute-start.5 = (bf16[256,2560]{1,0:T(8,128)(2,1)}, bf16[256,2560]{1,0:T(8,128)(2,1)S(1)}, u32[]{:S(2)}, u32[]{:S(2)}) collective-permute-start(bf16[256,2560]{1,0:T(8,128)(2,1)} %get-tuple-element.67), channel_id=1, source_target_pairs={{0,1},{1,0},{2,3},{3,2},{4,5},{5,4},{6,7},{7,6},{8,9},{9,8},{10,11... | collective-permute-start | bytes 3932168 | tf_op jit(solution)/shard_map/ppermute | solution.py:29
  39.0 28.4 %collective-permute-start.6 = (bf16[256,2560]{1,0:T(8,128)(2,1)}, bf16[256,2560]{1,0:T(8,128)(2,1)S(1)}, u32[]{:S(2)}, u32[]{:S(2)}) collective-permute-start(bf16[256,2560]{1,0:T(8,128)(2,1)} %get-tuple-element.68), channel_id=1, source_target_pairs={{0,1},{1,0},{2,3},{3,2},{4,5},{5,4},{6,7},{7,6},{8,9},{9,8},{10,11... | collective-permute-start | bytes 3932168 | tf_op jit(solution)/shard_map/ppermute | solution.py:29
  50.6 19.5 %collective-permute-start.7 = (bf16[256,2560]{1,0:T(8,128)(2,1)}, bf16[256,2560]{1,0:T(8,128)(2,1)S(1)}, u32[]{:S(2)}, u32[]{:S(2)}) collective-permute-start(bf16[256,2560]{1,0:T(8,128)(2,1)} %get-tuple-element.71), channel_id=1, source_target_pairs={{0,1},{1,0},{2,3},{3,2},{4,5},{5,4},{6,7},{7,6},{8,9},{9,8},{10,11... | collective-permute-start | bytes 3932168 | tf_op jit(solution)/shard_map/ppermute | solution.py:29
  64.1 44.5 %collective-permute-start.14 = (bf16[3,1024,256]{2,1,0:T(8,128)(2,1)}, bf16[3,1024,256]{2,1,0:T(8,128)(2,1)}, u32[]{:S(2)}, u32[]{:S(2)}) collective-permute-start(bf16[3,1024,256]{2,1,0:T(8,128)(2,1)} %collective-permute-done.4.refs_3_), channel_id=1, source_target_pairs={{0,16},{1,17},{2,18},{3,19},{4,20},{5,21},{6,22},{7,23},{8,24},{9,... | collective-permute-start | bytes 4718600 | tf_op jit(solution)/shard_map/ppermute | solution.py:29
  64.1 26.0 %collective-permute-start.9 = (bf16[2,1024,256]{2,1,0:T(8,128)(2,1)}, bf16[2,1024,256]{2,1,0:T(8,128)(2,1)}, u32[]{:S(2)}, u32[]{:S(2)}) collective-permute-start(bf16[2,1024,256]{2,1,0:T(8,128)(2,1)} %get-tuple-element.98.refs_0_), channel_id=1, source_target_pairs={{0,48},{1,49},{2,50},{3,51},{4,52},{5,53},{6,54},{7,55},{8,56},{9,... | collective-permute-start | bytes 3145736 | tf_op jit(solution)/shard_map/ppermute | solution.py:29
  68.5 15.7 %collective-permute-start.10 = (bf16[64,2560]{1,0:T(8,128)(2,1)S(1)}, bf16[64,2560]{1,0:T(8,128)(2,1)S(1)}, u32[]{:S(2)}, u32[]{:S(2)}) collective-permute-start(bf16[64,2560]{1,0:T(8,128)(2,1)S(1)} %get-tuple-element.78), channel_id=1, source_target_pairs={{0,2},{1,3},{2,4},{3,5},{4,6},{5,7},{6,0},{7,1},{8,10},{9,11},{10,... | collective-permute-start | bytes 983048 | tf_op jit(solution)/shard_map/ppermute | solution.py:29
  70.1 16.5 %collective-permute-start.11 = (bf16[64,2560]{1,0:T(8,128)(2,1)S(1)}, bf16[64,2560]{1,0:T(8,128)(2,1)S(1)}, u32[]{:S(2)}, u32[]{:S(2)}) collective-permute-start(bf16[64,2560]{1,0:T(8,128)(2,1)S(1)} %get-tuple-element.79), channel_id=1, source_target_pairs={{0,6},{1,7},{2,0},{3,1},{4,2},{5,3},{6,4},{7,5},{8,14},{9,15},{10,... | collective-permute-start | bytes 983048 | tf_op jit(solution)/shard_map/ppermute | solution.py:29
  73.8 46.6 %collective-permute-start.15 = (bf16[256,2560]{1,0:T(8,128)(2,1)}, bf16[256,2560]{1,0:T(8,128)(2,1)S(1)}, u32[]{:S(2)}, u32[]{:S(2)}) collective-permute-start(bf16[256,2560]{1,0:T(8,128)(2,1)} %get-tuple-element.86), channel_id=1, source_target_pairs={{0,8},{1,9},{2,10},{3,11},{4,12},{5,13},{6,14},{7,15},{8,0},{9,1},... | collective-permute-start | bytes 3932168 | tf_op jit(solution)/shard_map/ppermute | solution.py:29
  86.8 18.3 %collective-permute-start.12 = (bf16[128,2560]{1,0:T(8,128)(2,1)S(1)}, bf16[128,2560]{1,0:T(8,128)(2,1)S(1)}, u32[]{:S(2)}, u32[]{:S(2)}) collective-permute-start(bf16[128,2560]{1,0:T(8,128)(2,1)S(1)} %get-tuple-element.80), channel_id=1, source_target_pairs={{0,2},{1,3},{2,4},{3,5},{4,6},{5,7},{6,0},{7,1},{8,10},{9,11},{10,... | collective-permute-start | bytes 1966088 | tf_op jit(solution)/shard_map/ppermute | solution.py:29
  88.4 19.4 %collective-permute-start.13 = (bf16[128,2560]{1,0:T(8,128)(2,1)S(1)}, bf16[128,2560]{1,0:T(8,128)(2,1)S(1)}, u32[]{:S(2)}, u32[]{:S(2)}) collective-permute-start(bf16[128,2560]{1,0:T(8,128)(2,1)S(1)} %get-tuple-element.81), channel_id=1, source_target_pairs={{0,6},{1,7},{2,0},{3,1},{4,2},{5,3},{6,4},{7,5},{8,14},{9,15},{10,... | collective-permute-start | bytes 1966088 | tf_op jit(solution)/shard_map/ppermute | solution.py:29
  90.1 46.7 %collective-permute-start.20 = (bf16[2,1024,256]{2,1,0:T(8,128)(2,1)}, bf16[2,1024,256]{2,1,0:T(8,128)(2,1)}, u32[]{:S(2)}, u32[]{:S(2)}) collective-permute-start(bf16[2,1024,256]{2,1,0:T(8,128)(2,1)} %collective-permute-done.9.refs_1_), channel_id=1, source_target_pairs={{0,48},{1,49},{2,50},{3,51},{4,52},{5,53},{6,54},{7,55},{8,56},{9,... | collective-permute-start | bytes 3145736 | tf_op jit(solution)/shard_map/ppermute | solution.py:29
  105.9 30.8 %collective-permute-start.21 = (bf16[2,1024,256]{2,1,0:T(8,128)(2,1)}, bf16[2,1024,256]{2,1,0:T(8,128)(2,1)}, u32[]{:S(2)}, u32[]{:S(2)}) collective-permute-start(bf16[2,1024,256]{2,1,0:T(8,128)(2,1)} %get-tuple-element.98.refs_0_), channel_id=1, source_target_pairs={{0,16},{1,17},{2,18},{3,19},{4,20},{5,21},{6,22},{7,23},{8,24},{9,... | collective-permute-start | bytes 3145736 | tf_op jit(solution)/shard_map/ppermute | solution.py:29
  117.0 16.4 %collective-permute-start.18 = (bf16[3,320,256]{2,1,0:T(8,128)(2,1)}, bf16[3,320,256]{2,1,0:T(8,128)(2,1)}, u32[]{:S(2)}, u32[]{:S(2)}) collective-permute-start(bf16[3,320,256]{2,1,0:T(8,128)(2,1)} %get-tuple-element.83), channel_id=1, source_target_pairs={{0,8},{1,9},{2,10},{3,11},{4,12},{5,13},{6,14},{7,15},{8,64},{9,65... | collective-permute-start | bytes 1474568 | tf_op jit(solution)/shard_map/ppermute | solution.py:29
  118.6 14.8 %collective-permute-start.19 = (bf16[3,320,256]{2,1,0:T(8,128)(2,1)}, bf16[3,320,256]{2,1,0:T(8,128)(2,1)}, u32[]{:S(2)}, u32[]{:S(2)}) collective-permute-start(bf16[3,320,256]{2,1,0:T(8,128)(2,1)} %get-tuple-element.84), channel_id=1, source_target_pairs={{0,72},{1,73},{2,74},{3,75},{4,76},{5,77},{6,78},{7,79},{8,0},{9,1... | collective-permute-start | bytes 1474568 | tf_op jit(solution)/shard_map/ppermute | solution.py:29
  133.5 24.3 %collective-permute-start.22 = (bf16[3,320,256]{2,1,0:T(8,128)(2,1)}, bf16[3,320,256]{2,1,0:T(8,128)(2,1)S(1)}, u32[]{:S(2)}, u32[]{:S(2)}) collective-permute-start(bf16[3,320,256]{2,1,0:T(8,128)(2,1)} %collective-permute-done.18), channel_id=1, source_target_pairs={{0,8},{1,9},{2,10},{3,11},{4,12},{5,13},{6,14},{7,15},{8,64},{9,65... | collective-permute-start | bytes 1474568 | tf_op jit(solution)/shard_map/ppermute | solution.py:29
  133.8 25.5 %collective-permute-start.23 = (bf16[3,320,256]{2,1,0:T(8,128)(2,1)}, bf16[3,320,256]{2,1,0:T(8,128)(2,1)S(1)}, u32[]{:S(2)}, u32[]{:S(2)}) collective-permute-start(bf16[3,320,256]{2,1,0:T(8,128)(2,1)} %collective-permute-done.19), channel_id=1, source_target_pairs={{0,72},{1,73},{2,74},{3,75},{4,76},{5,77},{6,78},{7,79},{8,0},{9,1... | collective-permute-start | bytes 1474568 | tf_op jit(solution)/shard_map/ppermute | solution.py:29
  146.9 22.9 %collective-permute-start.26 = (bf16[64,2560]{1,0:T(8,128)(2,1)S(1)}, bf16[64,2560]{1,0:T(8,128)(2,1)S(1)}, u32[]{:S(2)}, u32[]{:S(2)}) collective-permute-start(bf16[64,2560]{1,0:T(8,128)(2,1)S(1)} %get-tuple-element.104), channel_id=1, source_target_pairs={{0,8},{1,9},{2,10},{3,11},{4,12},{5,13},{6,14},{7,15},{8,0},{9,1},... | collective-permute-start | bytes 983048 | tf_op jit(solution)/shard_map/ppermute | solution.py:29
  153.9 15.9 %collective-permute-start.24 = (bf16[64,2560]{1,0:T(8,128)(2,1)S(1)}, bf16[64,2560]{1,0:T(8,128)(2,1)S(1)}, u32[]{:S(2)}, u32[]{:S(2)}) collective-permute-start(bf16[64,2560]{1,0:T(8,128)(2,1)S(1)} %get-tuple-element.94), channel_id=1, source_target_pairs={{0,2},{1,3},{2,4},{3,5},{4,6},{5,7},{6,0},{7,1},{8,10},{9,11},{10,... | collective-permute-start | bytes 983048 | tf_op jit(solution)/shard_map/ppermute | solution.py:29
  154.7 15.1 %collective-permute-start.25 = (bf16[64,2560]{1,0:T(8,128)(2,1)S(1)}, bf16[64,2560]{1,0:T(8,128)(2,1)S(1)}, u32[]{:S(2)}, u32[]{:S(2)}) collective-permute-start(bf16[64,2560]{1,0:T(8,128)(2,1)S(1)} %get-tuple-element.95), channel_id=1, source_target_pairs={{0,6},{1,7},{2,0},{3,1},{4,2},{5,3},{6,4},{7,5},{8,14},{9,15},{10,... | collective-permute-start | bytes 983048 | tf_op jit(solution)/shard_map/ppermute | solution.py:29
  157.8 14.2 %collective-permute-start.28 = (bf16[2,320,256]{2,1,0:T(8,128)(2,1)}, bf16[2,320,256]{2,1,0:T(8,128)(2,1)S(1)}, u32[]{:S(2)}, u32[]{:S(2)}) collective-permute-start(bf16[2,320,256]{2,1,0:T(8,128)(2,1)} %collective-permute-done.27), channel_id=1, source_target_pairs={{0,8},{1,9},{2,10},{3,11},{4,12},{5,13},{6,14},{7,15},{8,64},{9,65... | collective-permute-start | bytes 983048 | tf_op jit(solution)/shard_map/ppermute | solution.py:29
  (23 other events, 195.7 us)
Sparse Core Ops, SparseCore 0:
  26.0 73.1 all-gather.2

commit v2 on v1

--- a/solution.py
+++ b/solution.py
@@ -41,7 +41,7 @@
     return ref[...].astype(F32)
 
 
-def small(kernel, outs, *values, scratch=()):
+def small(kernel, outs, *values, scratch=(), lasts=1.2):
     return pl.pallas_call(
         kernel,
         grid=(1,),
@@ -50,7 +50,7 @@
         out_shape=outs,
         scratch_shapes=scratch,
         compiler_params=FEW,
-        cost_estimate=lasting(1.2),
+        cost_estimate=lasting(lasts),
     )(*values)
 
 
@@ -80,7 +80,7 @@
             scratch_shapes=[pltpu.VMEM((64, 5120), F32)],
         ),
         out_shape=[like(64, 1280)] * 4,
-        compiler_params=FEW,
+        compiler_params=ROOM,
         cost_estimate=lasting(1.2),
     )(starts, rows, gain)
 
@@ -228,53 +228,54 @@
         right = jnp.concatenate([piece[0, b * 64 : b * 64 + 64, :] for b in blocks for piece in pieces], axis=0)
         term = jnp.dot(left, right, preferred_element_type=F32)
         total = term if total is None else total + term
-    if task == "send":
-        refs[0][0] = total[:320].astype(BF16)
-        refs[1][0] = total[320:].astype(BF16)
-    elif task == "keep":
-        refs[0][0] = total.astype(BF16)
-    else:
-        add_halves(refs[2], total, refs[0], refs[1])
-
-
-def weight(task, columns, pieces, other=()):
+    if task != "send":
+        refs[0][0] = total[:640].astype(BF16)
+    if task != "keep":
+        rows = total.shape[0]
+        refs[-2][0] = total[rows - 640 : rows - 320].astype(BF16)
+        refs[-1][0] = total[rows - 320 :].astype(BF16)
+
+
+def weight(task, columns, pieces):
     steps = pieces[0].shape[0]
     half = pl.BlockSpec((1, 320, 256), lambda i: (i, 0, 0))
-    if task == "send":
-        outs, shapes = [half, half], [like(steps, 320, 256)] * 2
-    elif task == "keep":
+    taken = pl.BlockSpec((16, 640, 256), lambda i: (0, int(task == "send"), 0))
+    if task == "both":
+        taken = pl.BlockSpec((16, 1280, 256), lambda i: (0, 0, 0))
+    outs, shapes = [], []
+    if task != "send":
         outs, shapes = [pl.BlockSpec((1, 640, 256), lambda i: (i, 0, 0))], [like(steps, 640, 256)]
-    else:
-        outs, shapes = [pl.BlockSpec((640, 256), lambda i: (0, 2 + i))], [like(640, 1280)]
+    if task != "keep":
+        outs, shapes = outs + [half, half], shapes + [like(steps, 320, 256)] * 2
     return pl.pallas_call(
         functools.partial(weight_kernel, task),
         grid=(steps,),
-        in_specs=[pl.BlockSpec((16, 640, 256), lambda i: (0, int(task == "send"), 0))]
-        + [pl.BlockSpec((1, 1024, 256), lambda i: (i, 0, 0))] * 4
-        + [half] * len(other),
+        in_specs=[taken]
+        + [pl.BlockSpec((1, 1024, 256), lambda i: (i, 0, 0))] * 4,
         out_specs=outs,
         out_shape=shapes,
         compiler_params=ROOM,
         cost_estimate=lasting(1.5 + 1.8 * steps),
-    )(columns, *pieces, *other)
-
-
-def put_kernel(keep_ref, up_ref, down_ref, given_ref, out_ref):
-    add_halves(out_ref, keep_ref[0], up_ref, down_ref)
-
-
-def put(keep, up, down, given):
+    )(columns, *pieces)
+
+
+def put_kernel(keep_ref, up_ref, down_ref, *refs):
+    add_halves(refs[-1], keep_ref[0], up_ref, down_ref)
+
+
+def put(keep, up, down, place, given=()):
     half = pl.BlockSpec((1, 320, 256), lambda i: (i, 0, 0))
     return pl.pallas_call(
         put_kernel,
-        grid=(2,),
-        in_specs=[pl.BlockSpec((1, 640, 256), lambda i: (i, 0, 0)), half, half, pl.BlockSpec(memory_space=pl.ANY)],
-        out_specs=pl.BlockSpec((640, 256), lambda i: (0, i)),
+        grid=(keep.shape[0],),
+        in_specs=[pl.BlockSpec((1, 640, 256), lambda i: (i, 0, 0)), half, half]
+        + [pl.BlockSpec(memory_space=pl.ANY)] * len(given),
+        out_specs=pl.BlockSpec((640, 256), lambda i: (0, place + i)),
         out_shape=like(640, 1280),
-        input_output_aliases={3: 0},
-        compiler_params=ROOM,
+        input_output_aliases={3: 0} if given else {},
+        compiler_params=FEW,
         cost_estimate=lasting(2),
-    )(keep, up, down, given)
+    )(keep, up, down, *given)
 
 
 def local(inputs, norm_gain, w_in, pre_gelu, grad_hidden, grad_out):
@@ -306,33 +307,34 @@
     keep, send = added(add_left_kernel, [256, 256], after(own_left, own_right), far_left)
     send = moved(send, y_lo=1)
 
-    first_far = moved(first[1], z=1)
-    second_next = moved(after(chunks[1], *first), z=-1)
-    ahead, behind = small(join_kernel, [like(128, 2560)] * 2, next_right, last_right, front, rear)
+    first_far = moved(after(first[1], own_right), z=1)
+    second_next = moved(after(chunks[1], *first, own_right), z=-1)
+    next_right = after(next_right, keep)
+    ahead, behind = small(join_kernel, [like(128, 2560)] * 2, next_right, last_right, front, rear, lasts=1.2)
     second_far = moved(after(second_next, ahead), z=-1)
-    second_last = moved(after(chunks[1], second_next, ahead), z=1)
+    second_last = moved(after(chunks[1], second_next, ahead, first_far), z=1)
     pieces = [[chunks[0], first[0], first_far, first[1]], [chunks[1], second_next, second_far, second_last]]
     ahead, behind = moved(ahead, x=1), moved(behind, x=-1)
 
-    sent = weight("send", after(columns, second_next, ahead, behind), pieces[0])
+    kept, *sent = weight("both", after(columns, second_next, ahead, behind), pieces[0])
     hop = [moved(sent[0], y=1), moved(sent[1], y=-1)]
-    other = [moved(hop[0], y=1), moved(hop[1], y=-1)]
-
+
+    outs = [like(count, 2560) for count in (32, 32, 64, 64, 64)]
+    keep = after(keep, *sent, second_far)
+    front, rear, next_left, last_left, own_left = small(split_left_kernel, outs, keep, send)
+    front, rear = moved(front, x=1), moved(rear, x=-1)
+
+    kept_1, *sent = weight("both", after(columns, own_left), pieces[1])
+    other = [moved(after(rows, kept_1), y=way) for rows, way in zip(hop, (1, -1))]
+    next_left = after(next_left, *sent)
+    sides = small(join_kernel, [like(64, 2560)] * 2, next_left, last_left, front, rear)
     right_keep, right_send = small(
         right_sum_kernel, [like(64, 2560, kind=F32), like(64, 2560)], after(own_right, *sent), ahead, behind
     )
     right_send = moved(right_send, y_lo=1)
-    outs = [like(count, 2560) for count in (32, 32, 64, 64, 64)]
-    keep = after(keep, *sent)
-    front, rear, next_left, last_left, own_left = small(split_left_kernel, outs, keep, send)
-    front, rear = moved(front, x=1), moved(rear, x=-1)
-    sides = small(join_kernel, [like(64, 2560)] * 2, next_left, last_left, front, rear)
     ahead, behind = moved(sides[0], x=1), moved(sides[1], x=-1)
-
-    sent = weight("send", after(columns, right_keep, *sides, *hop), pieces[1])
     hop = [moved(sent[0], y=1), moved(sent[1], y=-1)]
-    (kept,) = weight("keep", after(columns, *sent), pieces[1])
-    (grad_w_in,) = weight("put", after(columns, kept), pieces[0], other)
+    grad_w_in = put(after(kept, kept_1), *other, 2)
     (grad_in,) = small(
         end_kernel,
         [like(64, 5120)],
@@ -346,7 +348,7 @@
         right_send,
         scratch=[pltpu.VMEM((64, 5120), F32)],
     )
-    grad_w_in = put(after(kept, grad_in), moved(hop[0], y=1), moved(hop[1], y=-1), grad_w_in)
+    grad_w_in = put(after(kept_1, grad_in), moved(hop[0], y=1), moved(hop[1], y=-1), 0, [grad_w_in])
     return (grad_in, grad_w_in)
 
 

time: 183 us -> 181 us (0.989)
  waiting for transfers between devices: 46.4 us -> 50.2 us
  Pallas kernels: 71.5 us -> 68.9 us
  local copies, waits for them, and re-layouts: 4.97 us -> 2.45 us
    pallas_call x4 -> x2, Pallas kernels: 31.1 us -> 25.9 us  [weight(): pl.pallas_call(functools.partial(weight_kernel, task), grid=(steps,), in_...]
    ppermute x31, waiting for transfers between devices: 46.4 us -> 50.2 us  [moved(): return lax.ppermute(value, AXES, pairs)]
    unnamed x30, local copies, waits for them, and re-layouts: 4.97 us -> 2.45 us
    pallas_call x1, Pallas kernels: 1.11 us -> 3.12 us  [normed_blocks(): pl.pallas_call(normed_kernel, grid_spec=pltpu.PrefetchScalarGridSpec(num_...]
  transfers between devices with their start and end apart: 32 -> 32, of which waited for: 9 -> 13; matrix products, arithmetic and copies ran while one was open for 0% -> 0% of each run, Pallas kernels for 37% -> 35%
where the time goes in v2:
time: 181 us; the launch traced here: 180 us
  Pallas kernels  68.9 us (38%)
  waiting for transfers between devices  50.2 us (28%)
  starting transfers between devices  43.4 us (24%)
  between operations  14.2 us (8%)
  local copies, waits for them, and re-layouts  2.45 us (1%)
    ppermute x31, waiting for transfers between devices, moved(): return lax.ppermute(value, AXES, pairs)  50.2 us
    ppermute x31, starting transfers between devices, moved(): return lax.ppermute(value, AXES, pairs)  43.4 us
    pallas_call x2, Pallas kernels, weight(): pl.pallas_call(functools.partial(weight_kernel, task), grid=(steps,), in_...  25.9 us
    pallas_call x2, Pallas kernels, back(): pl.pallas_call(back_kernel, grid=(5,), in_specs=[pl.BlockSpec((1024, 1280...  22.1 us
    pallas_call x1, Pallas kernels, grad_pre_of(): pl.pallas_call(slope_kernel, grid_spec=pltpu.PrefetchScalarGridSpec(num_s...  8.05 us
    pallas_call x6, Pallas kernels, small(): pl.pallas_call(kernel, grid=(1,), in_specs=[pl.BlockSpec(value.shape, lam...  3.99 us
  transfers between devices with their start and end apart: 32, of which 13 were waited for; matrix products, arithmetic and copies ran while one was open for 0% of the time, Pallas kernels for 35%

profile of v2, /device:TPU:0, one launch (start us, length us, event | category | flops | bytes accessed | tf_op | source)
XLA Modules:
  0.0 180.4 jit_solution(15749777948123147083)
XLA Ops:
  7.8 3.1 %shard_map.77 = (bf16[64,1280]{1,0:T(8,128)(2,1)}, bf16[64,1280]{1,0:T(8,128)(2,1)}, bf16[64,1280]{1,0:T(8,128)(2,1)}, bf16[64,1280]{1,0:T(8,128)(2,1)}) custom-call(s32[8]{0:T(128)} %fusion.15.starts, bf16[64,5120]{1,0:T(8,128)(2,1)} %rows_ref.3, f32[1,5120]{1,0:T(1,128)} %bitcast.2), custom_call_target="tpu_custom_call" | custom-call | flops 660000000 | bytes 65536 | tf_op jit(solution)/shard_map/pallas_call | solution.py:73
  10.9 4.1 %collective-permute-start = (bf16[64,1280]{1,0:T(8,128)(2,1)}, bf16[64,1280]{1,0:T(8,128)(2,1)S(1)}, u32[]{:S(2)}, u32[]{:S(2)}) collective-permute-start(bf16[64,1280]{1,0:T(8,128)(2,1)} %get-tuple-element.63), channel_id=1, source_target_pairs={{0,48},{1,49},{2,50},{3,51},{4,52},{5,53},{6,54},{7,55},{8,56},{9,... | collective-permute-start | bytes 491528 | tf_op jit(solution)/shard_map/ppermute | solution.py:29
  16.8 8.1 %shard_map.78 = (bf16[3,1024,256]{2,1,0:T(8,128)(2,1)}, bf16[2,1024,256]{2,1,0:T(8,128)(2,1)}, bf16[1024,1280]{1,0:T(8,128)(2,1)}) custom-call(s32[16]{0:T(128)} %fusion.places, bf16[1024,1280]{1,0:T(8,128)(2,1)} %pre_ref.1, bf16[1024,1280]{1,0:T(8,128)(2,1)} %hidden_ref.1), custom_call_target="tpu_custom_call" | custom-call | flops 2750000128 | bytes 65536 | tf_op jit(solution)/shard_map/pallas_call | solution.py:117
  28.8 11.0 %shard_map.80 = (bf16[512,2560]{1,0:T(8,128)(2,1)}, bf16[256,2560]{1,0:T(8,128)(2,1)}, bf16[256,2560]{1,0:T(8,128)(2,1)}) custom-call(bf16[1024,1280]{1,0:T(8,128)(2,1)} %get-tuple-element.69.rows_ref, bf16[5120,1280]{1,0:T(8,128)(2,1)} %w_ref.3), custom_call_target="tpu_custom_call" | custom-call | flops 550000000 | bytes 65536 | tf_op jit(solution)/shard_map/pallas_call | solution.py:141
  40.3 11.1 %shard_map.81 = (bf16[512,2560]{1,0:T(8,128)(2,1)}, bf16[256,2560]{1,0:T(8,128)(2,1)}, bf16[256,2560]{1,0:T(8,128)(2,1)}) custom-call(bf16[1024,1280]{1,0:T(8,128)(2,1)} %get-tuple-element.69.rows_ref, bf16[5120,1280]{1,0:T(8,128)(2,1)} %w_ref.3), custom_call_target="tpu_custom_call" | custom-call | flops 550000000 | bytes 65536 | tf_op jit(solution)/shard_map/pallas_call | solution.py:141
  51.4 11.6 %collective-permute-done.3.refs_1_ = bf16[3,1024,256]{2,1,0:T(8,128)(2,1)} collective-permute-done((bf16[3,1024,256]{2,1,0:T(8,128)(2,1)}, bf16[3,1024,256]{2,1,0:T(8,128)(2,1)}, u32[]{:S(2)}, u32[]{:S(2)}) %collective-permute-start.3) | collective-permute-done | bytes 1572896 | tf_op jit(solution)/shard_map/ppermute | solution.py:29
  63.0 1.9 %collective-permute-done.4.refs_3_ = bf16[3,1024,256]{2,1,0:T(8,128)(2,1)} collective-permute-done((bf16[3,1024,256]{2,1,0:T(8,128)(2,1)}, bf16[3,1024,256]{2,1,0:T(8,128)(2,1)}, u32[]{:S(2)}, u32[]{:S(2)}) %collective-permute-start.4) | collective-permute-done | bytes 1572896 | tf_op jit(solution)/shard_map/ppermute | solution.py:29
  66.2 3.2 %collective-permute-start.9 = (bf16[2,1024,256]{2,1,0:T(8,128)(2,1)}, bf16[2,1024,256]{2,1,0:T(8,128)(2,1)}, u32[]{:S(2)}, u32[]{:S(2)}) collective-permute-start(bf16[2,1024,256]{2,1,0:T(8,128)(2,1)} %get-tuple-element.99.refs_0_), channel_id=1, source_target_pairs={{0,48},{1,49},{2,50},{3,51},{4,52},{5,53},{6,54},{7,55},{8,56},{9,... | collective-permute-start | bytes 3145736 | tf_op jit(solution)/shard_map/ppermute | solution.py:29
  72.7 2.0 %shard_map.83 = (bf16[256,2560]{1,0:T(8,128)(2,1)S(1)}, bf16[256,2560]{1,0:T(8,128)(2,1)}) custom-call(bf16[512,2560]{1,0:T(8,128)(2,1)S(1)} %copy-done, bf16[256,2560]{1,0:T(8,128)(2,1)S(1)} %collective-permute-done.7.refs_0_, bf16[256,2560]{1,0:T(8,128)(2,1)S(1)} %collective-permute-done.8.refs_1_), custom_call_target="tpu_custom_call" | custom-call | flops 550000000 | bytes 65536 | tf_op jit(solution)/shard_map/pallas_call | solution.py:173
  76.2 8.8 %collective-permute-done.10.front_ref = bf16[64,2560]{1,0:T(8,128)(2,1)S(1)} collective-permute-done((bf16[64,2560]{1,0:T(8,128)(2,1)S(1)}, bf16[64,2560]{1,0:T(8,128)(2,1)S(1)}, u32[]{:S(2)}, u32[]{:S(2)}) %collective-permute-start.10) | collective-permute-done | bytes 327712 | tf_op jit(solution)/shard_map/ppermute | solution.py:29
  85.1 2.4 %collective-permute-done.11.rear_ref = bf16[64,2560]{1,0:T(8,128)(2,1)S(1)} collective-permute-done((bf16[64,2560]{1,0:T(8,128)(2,1)S(1)}, bf16[64,2560]{1,0:T(8,128)(2,1)S(1)}, u32[]{:S(2)}, u32[]{:S(2)}) %collective-permute-start.11) | collective-permute-done | bytes 327712 | tf_op jit(solution)/shard_map/ppermute | solution.py:29
  90.9 3.5 %collective-permute-start.15 = (bf16[2,1024,256]{2,1,0:T(8,128)(2,1)}, bf16[2,1024,256]{2,1,0:T(8,128)(2,1)}, u32[]{:S(2)}, u32[]{:S(2)}) collective-permute-start(bf16[2,1024,256]{2,1,0:T(8,128)(2,1)} %collective-permute-done.9.refs_1_), channel_id=1, source_target_pairs={{0,48},{1,49},{2,50},{3,51},{4,52},{5,53},{6,54},{7,55},{8,56},{9,... | collective-permute-start | bytes 3145736 | tf_op jit(solution)/shard_map/ppermute | solution.py:29
  94.4 8.2 %collective-permute-done.14.refs_2_ = bf16[3,1024,256]{2,1,0:T(8,128)(2,1)S(1)} collective-permute-done((bf16[3,1024,256]{2,1,0:T(8,128)(2,1)}, bf16[3,1024,256]{2,1,0:T(8,128)(2,1)S(1)}, u32[]{:S(2)}, u32[]{:S(2)}) %collective-permute-start.14) | collective-permute-done | bytes 1572896 | tf_op jit(solution)/shard_map/ppermute | solution.py:29
  102.6 3.3 %collective-permute-done.12.ahead_ref = bf16[128,2560]{1,0:T(8,128)(2,1)S(1)} collective-permute-done((bf16[128,2560]{1,0:T(8,128)(2,1)S(1)}, bf16[128,2560]{1,0:T(8,128)(2,1)S(1)}, u32[]{:S(2)}, u32[]{:S(2)}) %collective-permute-start.12) | collective-permute-done | bytes 655392 | tf_op jit(solution)/shard_map/ppermute | solution.py:29
  108.9 14.3 %shard_map.85 = (bf16[3,640,256]{2,1,0:T(8,128)(2,1)}, bf16[3,320,256]{2,1,0:T(8,128)(2,1)}, bf16[3,320,256]{2,1,0:T(8,128)(2,1)}) custom-call(bf16[16,1280,256]{2,1,0:T(8,128)(2,1)} %bitcast.4, bf16[3,1024,256]{2,1,0:T(8,128)(2,1)} %get-tuple-element.71.refs_0_, bf16[3,1024,256]{2,1,0:T(8,128)(2,1)} %collective-permute-done.3.refs_1_, ...), custom_call_target="tpu_custom_call" | custom-call | flops 3795000064 | bytes 65536 | tf_op jit(solution)/shard_map/pallas_call | solution.py:250
  127.6 11.6 %shard_map.87 = (bf16[2,640,256]{2,1,0:T(8,128)(2,1)}, bf16[2,320,256]{2,1,0:T(8,128)(2,1)}, bf16[2,320,256]{2,1,0:T(8,128)(2,1)}) custom-call(bf16[16,1280,256]{2,1,0:T(8,128)(2,1)} %bitcast.5, bf16[2,1024,256]{2,1,0:T(8,128)(2,1)} %get-tuple-element.99.refs_0_, bf16[2,1024,256]{2,1,0:T(8,128)(2,1)} %collective-permute-done.9.refs_1_, ...), custom_call_target="tpu_custom_call" | custom-call | flops 2804999936 | bytes 65536 | tf_op jit(solution)/shard_map/pallas_call | solution.py:250
  140.2 2.3 %collective-permute-start.21 = (bf16[3,320,256]{2,1,0:T(8,128)(2,1)}, bf16[3,320,256]{2,1,0:T(8,128)(2,1)S(1)}, u32[]{:S(2)}, u32[]{:S(2)}) collective-permute-start(bf16[3,320,256]{2,1,0:T(8,128)(2,1)} %collective-permute-done.20), channel_id=1, source_target_pairs={{0,72},{1,73},{2,74},{3,75},{4,76},{5,77},{6,78},{7,79},{8,0},{9,1... | collective-permute-start | bytes 1474568 | tf_op jit(solution)/shard_map/ppermute | solution.py:29
  143.9 3.2 %collective-permute-start.29 = (bf16[2,320,256]{2,1,0:T(8,128)(2,1)}, bf16[2,320,256]{2,1,0:T(8,128)(2,1)S(1)}, u32[]{:S(2)}, u32[]{:S(2)}) collective-permute-start(bf16[2,320,256]{2,1,0:T(8,128)(2,1)} %get-tuple-element.107), channel_id=1, source_target_pairs={{0,72},{1,73},{2,74},{3,75},{4,76},{5,77},{6,78},{7,79},{8,0},{9,1... | collective-permute-start | bytes 983048 | tf_op jit(solution)/shard_map/ppermute | solution.py:29
  147.2 1.8 %collective-permute-done.22.front_ref = bf16[32,2560]{1,0:T(8,128)(2,1)S(1)} collective-permute-done((bf16[32,2560]{1,0:T(8,128)(2,1)S(1)}, bf16[32,2560]{1,0:T(8,128)(2,1)S(1)}, u32[]{:S(2)}, u32[]{:S(2)}) %collective-permute-start.22) | collective-permute-done | bytes 163872 | tf_op jit(solution)/shard_map/ppermute | solution.py:29
  150.9 3.4 %collective-permute-done.23.rear_ref = bf16[32,2560]{1,0:T(8,128)(2,1)S(1)} collective-permute-done((bf16[32,2560]{1,0:T(8,128)(2,1)S(1)}, bf16[32,2560]{1,0:T(8,128)(2,1)S(1)}, u32[]{:S(2)}, u32[]{:S(2)}) %collective-permute-start.23) | collective-permute-done | bytes 163872 | tf_op jit(solution)/shard_map/ppermute | solution.py:29
  154.4 4.8 %collective-permute-done.27 = bf16[2,320,256]{2,1,0:T(8,128)(2,1)S(1)} collective-permute-done((bf16[2,320,256]{2,1,0:T(8,128)(2,1)}, bf16[2,320,256]{2,1,0:T(8,128)(2,1)S(1)}, u32[]{:S(2)}, u32[]{:S(2)}) %collective-permute-start.27) | collective-permute-done | bytes 327712 | tf_op jit(solution)/shard_map/ppermute | solution.py:29
  161.5 2.9 %collective-permute-start.25 = (bf16[64,2560]{1,0:T(8,128)(2,1)S(1)}, bf16[64,2560]{1,0:T(8,128)(2,1)S(1)}, u32[]{:S(2)}, u32[]{:S(2)}) collective-permute-start(bf16[64,2560]{1,0:T(8,128)(2,1)S(1)} %get-tuple-element.113), channel_id=1, source_target_pairs={{0,6},{1,7},{2,0},{3,1},{4,2},{5,3},{6,4},{7,5},{8,14},{9,15},{10,... | collective-permute-start | bytes 983048 | tf_op jit(solution)/shard_map/ppermute | solution.py:29
  164.8 2.7 %collective-permute-start.30 = (bf16[2,320,256]{2,1,0:T(8,128)(2,1)S(1)}, bf16[2,320,256]{2,1,0:T(8,128)(2,1)S(1)}, u32[]{:S(2)}, u32[]{:S(2)}) collective-permute-start(bf16[2,320,256]{2,1,0:T(8,128)(2,1)S(1)} %collective-permute-done.29), channel_id=1, source_target_pairs={{0,72},{1,73},{2,74},{3,75},{4,76},{5,77},{6,78},{7,79},{8,0},{9,1... | collective-permute-start | bytes 983048 | tf_op jit(solution)/shard_map/ppermute | solution.py:29
  169.2 2.1 %shard_map.91 = bf16[64,5120]{1,0:T(8,128)(2,1)} custom-call(bf16[64,5120]{1,0:T(8,128)(2,1)S(1)} %copy-done.3, f32[1,5120]{1,0:T(1,128)S(1)} %bitcast.3, bf16[64,5120]{1,0:T(8,128)(2,1)S(1)} %copy-done.4, bf16[64,2560]{1,0:T(8,128)(2,1)S(1)} %get-tuple-element.104.own_ref, bf16[64,2560]{1,0:T(8,128)(2,1)S(1)} %collective-permute-done.24.ahead_ref, ...), custom_call_target="tpu_custom_call" | custom-call | flops 660000000 | bytes 65536 | tf_op jit(solution)/shard_map/pallas_call | solution.py:45
  (89 shorter events, 34.7 us)
Async XLA Ops:
  7.2 101.8 %all-gather.3.cloned.1.call-start = ((), (), s32[]{:S(2)}) async-start(), calls=%async_computation | async-start | bytes 11141120 | tf_op jit(solution)/shard_map/all_gather | solution.py:296
  10.9 14.0 %collective-permute-start = (bf16[64,1280]{1,0:T(8,128)(2,1)}, bf16[64,1280]{1,0:T(8,128)(2,1)S(1)}, u32[]{:S(2)}, u32[]{:S(2)}) collective-permute-start(bf16[64,1280]{1,0:T(8,128)(2,1)} %get-tuple-element.63), channel_id=1, source_target_pairs={{0,48},{1,49},{2,50},{3,51},{4,52},{5,53},{6,54},{7,55},{8,56},{9,... | collective-permute-start | bytes 491528 | tf_op jit(solution)/shard_map/ppermute | solution.py:29
  15.0 10.6 %collective-permute-start.2 = (bf16[64,1280]{1,0:T(8,128)(2,1)}, bf16[64,1280]{1,0:T(8,128)(2,1)S(1)}, u32[]{:S(2)}, u32[]{:S(2)}) collective-permute-start(bf16[64,1280]{1,0:T(8,128)(2,1)} %get-tuple-element.61), channel_id=1, source_target_pairs={{0,16},{1,17},{2,18},{3,19},{4,20},{5,21},{6,22},{7,23},{8,24},{9,... | collective-permute-start | bytes 491528 | tf_op jit(solution)/shard_map/ppermute | solution.py:29
  26.7 36.4 %collective-permute-start.3 = (bf16[3,1024,256]{2,1,0:T(8,128)(2,1)}, bf16[3,1024,256]{2,1,0:T(8,128)(2,1)}, u32[]{:S(2)}, u32[]{:S(2)}) collective-permute-start(bf16[3,1024,256]{2,1,0:T(8,128)(2,1)} %get-tuple-element.71.refs_0_), channel_id=1, source_target_pairs={{0,48},{1,49},{2,50},{3,51},{4,52},{5,53},{6,54},{7,55},{8,56},{9,... | collective-permute-start | bytes 4718600 | tf_op jit(solution)/shard_map/ppermute | solution.py:29
  28.1 36.8 %collective-permute-start.4 = (bf16[3,1024,256]{2,1,0:T(8,128)(2,1)}, bf16[3,1024,256]{2,1,0:T(8,128)(2,1)}, u32[]{:S(2)}, u32[]{:S(2)}) collective-permute-start(bf16[3,1024,256]{2,1,0:T(8,128)(2,1)} %get-tuple-element.71.refs_0_), channel_id=1, source_target_pairs={{0,16},{1,17},{2,18},{3,19},{4,20},{5,21},{6,22},{7,23},{8,24},{9,... | collective-permute-start | bytes 4718600 | tf_op jit(solution)/shard_map/ppermute | solution.py:29
  39.8 25.1 %collective-permute-start.5 = (bf16[256,2560]{1,0:T(8,128)(2,1)}, bf16[256,2560]{1,0:T(8,128)(2,1)S(1)}, u32[]{:S(2)}, u32[]{:S(2)}) collective-permute-start(bf16[256,2560]{1,0:T(8,128)(2,1)} %get-tuple-element.73), channel_id=1, source_target_pairs={{0,1},{1,0},{2,3},{3,2},{4,5},{5,4},{6,7},{7,6},{8,9},{9,8},{10,11... | collective-permute-start | bytes 3932168 | tf_op jit(solution)/shard_map/ppermute | solution.py:29
  39.8 25.1 %collective-permute-start.6 = (bf16[256,2560]{1,0:T(8,128)(2,1)}, bf16[256,2560]{1,0:T(8,128)(2,1)S(1)}, u32[]{:S(2)}, u32[]{:S(2)}) collective-permute-start(bf16[256,2560]{1,0:T(8,128)(2,1)} %get-tuple-element.74), channel_id=1, source_target_pairs={{0,1},{1,0},{2,3},{3,2},{4,5},{5,4},{6,7},{7,6},{8,9},{9,8},{10,11... | collective-permute-start | bytes 3932168 | tf_op jit(solution)/shard_map/ppermute | solution.py:29
  51.4 19.5 %collective-permute-start.7 = (bf16[256,2560]{1,0:T(8,128)(2,1)}, bf16[256,2560]{1,0:T(8,128)(2,1)S(1)}, u32[]{:S(2)}, u32[]{:S(2)}) collective-permute-start(bf16[256,2560]{1,0:T(8,128)(2,1)} %get-tuple-element.77), channel_id=1, source_target_pairs={{0,1},{1,0},{2,3},{3,2},{4,5},{5,4},{6,7},{7,6},{8,9},{9,8},{10,11... | collective-permute-start | bytes 3932168 | tf_op jit(solution)/shard_map/ppermute | solution.py:29
  66.1 36.5 %collective-permute-start.14 = (bf16[3,1024,256]{2,1,0:T(8,128)(2,1)}, bf16[3,1024,256]{2,1,0:T(8,128)(2,1)S(1)}, u32[]{:S(2)}, u32[]{:S(2)}) collective-permute-start(bf16[3,1024,256]{2,1,0:T(8,128)(2,1)} %collective-permute-done.4.refs_3_), channel_id=1, source_target_pairs={{0,16},{1,17},{2,18},{3,19},{4,20},{5,21},{6,22},{7,23},{8,24},{9,... | collective-permute-start | bytes 4718600 | tf_op jit(solution)/shard_map/ppermute | solution.py:29
  66.2 24.7 %collective-permute-start.9 = (bf16[2,1024,256]{2,1,0:T(8,128)(2,1)}, bf16[2,1024,256]{2,1,0:T(8,128)(2,1)}, u32[]{:S(2)}, u32[]{:S(2)}) collective-permute-start(bf16[2,1024,256]{2,1,0:T(8,128)(2,1)} %get-tuple-element.99.refs_0_), channel_id=1, source_target_pairs={{0,48},{1,49},{2,50},{3,51},{4,52},{5,53},{6,54},{7,55},{8,56},{9,... | collective-permute-start | bytes 3145736 | tf_op jit(solution)/shard_map/ppermute | solution.py:29
  69.4 15.6 %collective-permute-start.10 = (bf16[64,2560]{1,0:T(8,128)(2,1)S(1)}, bf16[64,2560]{1,0:T(8,128)(2,1)S(1)}, u32[]{:S(2)}, u32[]{:S(2)}) collective-permute-start(bf16[64,2560]{1,0:T(8,128)(2,1)S(1)} %get-tuple-element.85), channel_id=1, source_target_pairs={{0,2},{1,3},{2,4},{3,5},{4,6},{5,7},{6,0},{7,1},{8,10},{9,11},{10,... | collective-permute-start | bytes 983048 | tf_op jit(solution)/shard_map/ppermute | solution.py:29
  70.9 16.5 %collective-permute-start.11 = (bf16[64,2560]{1,0:T(8,128)(2,1)S(1)}, bf16[64,2560]{1,0:T(8,128)(2,1)S(1)}, u32[]{:S(2)}, u32[]{:S(2)}) collective-permute-start(bf16[64,2560]{1,0:T(8,128)(2,1)S(1)} %get-tuple-element.86), channel_id=1, source_target_pairs={{0,6},{1,7},{2,0},{3,1},{4,2},{5,3},{6,4},{7,5},{8,14},{9,15},{10,... | collective-permute-start | bytes 983048 | tf_op jit(solution)/shard_map/ppermute | solution.py:29
  74.7 51.9 %collective-permute-start.16 = (bf16[256,2560]{1,0:T(8,128)(2,1)}, bf16[256,2560]{1,0:T(8,128)(2,1)S(1)}, u32[]{:S(2)}, u32[]{:S(2)}) collective-permute-start(bf16[256,2560]{1,0:T(8,128)(2,1)} %get-tuple-element.95), channel_id=1, source_target_pairs={{0,8},{1,9},{2,10},{3,11},{4,12},{5,13},{6,14},{7,15},{8,0},{9,1},... | collective-permute-start | bytes 3932168 | tf_op jit(solution)/shard_map/ppermute | solution.py:29
  87.6 18.3 %collective-permute-start.12 = (bf16[128,2560]{1,0:T(8,128)(2,1)S(1)}, bf16[128,2560]{1,0:T(8,128)(2,1)S(1)}, u32[]{:S(2)}, u32[]{:S(2)}) collective-permute-start(bf16[128,2560]{1,0:T(8,128)(2,1)S(1)} %get-tuple-element.87), channel_id=1, source_target_pairs={{0,2},{1,3},{2,4},{3,5},{4,6},{5,7},{6,0},{7,1},{8,10},{9,11},{10,... | collective-permute-start | bytes 1966088 | tf_op jit(solution)/shard_map/ppermute | solution.py:29
  89.2 18.9 %collective-permute-start.13 = (bf16[128,2560]{1,0:T(8,128)(2,1)S(1)}, bf16[128,2560]{1,0:T(8,128)(2,1)S(1)}, u32[]{:S(2)}, u32[]{:S(2)}) collective-permute-start(bf16[128,2560]{1,0:T(8,128)(2,1)S(1)} %get-tuple-element.88), channel_id=1, source_target_pairs={{0,6},{1,7},{2,0},{3,1},{4,2},{5,3},{6,4},{7,5},{8,14},{9,15},{10,... | collective-permute-start | bytes 1966088 | tf_op jit(solution)/shard_map/ppermute | solution.py:29
  90.9 35.6 %collective-permute-start.15 = (bf16[2,1024,256]{2,1,0:T(8,128)(2,1)}, bf16[2,1024,256]{2,1,0:T(8,128)(2,1)}, u32[]{:S(2)}, u32[]{:S(2)}) collective-permute-start(bf16[2,1024,256]{2,1,0:T(8,128)(2,1)} %collective-permute-done.9.refs_1_), channel_id=1, source_target_pairs={{0,48},{1,49},{2,50},{3,51},{4,52},{5,53},{6,54},{7,55},{8,56},{9,... | collective-permute-start | bytes 3145736 | tf_op jit(solution)/shard_map/ppermute | solution.py:29
  102.6 25.0 %collective-permute-start.17 = (bf16[2,1024,256]{2,1,0:T(8,128)(2,1)}, bf16[2,1024,256]{2,1,0:T(8,128)(2,1)}, u32[]{:S(2)}, u32[]{:S(2)}) collective-permute-start(bf16[2,1024,256]{2,1,0:T(8,128)(2,1)} %get-tuple-element.99.refs_0_), channel_id=1, source_target_pairs={{0,16},{1,17},{2,18},{3,19},{4,20},{5,21},{6,22},{7,23},{8,24},{9,... | collective-permute-start | bytes 3145736 | tf_op jit(solution)/shard_map/ppermute | solution.py:29
  123.3 15.9 %collective-permute-start.18 = (bf16[3,320,256]{2,1,0:T(8,128)(2,1)}, bf16[3,320,256]{2,1,0:T(8,128)(2,1)}, u32[]{:S(2)}, u32[]{:S(2)}) collective-permute-start(bf16[3,320,256]{2,1,0:T(8,128)(2,1)} %get-tuple-element.91), channel_id=1, source_target_pairs={{0,8},{1,9},{2,10},{3,11},{4,12},{5,13},{6,14},{7,15},{8,64},{9,65... | collective-permute-start | bytes 1474568 | tf_op jit(solution)/shard_map/ppermute | solution.py:29
  124.8 15.4 %collective-permute-start.20 = (bf16[3,320,256]{2,1,0:T(8,128)(2,1)}, bf16[3,320,256]{2,1,0:T(8,128)(2,1)}, u32[]{:S(2)}, u32[]{:S(2)}) collective-permute-start(bf16[3,320,256]{2,1,0:T(8,128)(2,1)} %get-tuple-element.92), channel_id=1, source_target_pairs={{0,72},{1,73},{2,74},{3,75},{4,76},{5,77},{6,78},{7,79},{8,0},{9,1... | collective-permute-start | bytes 1474568 | tf_op jit(solution)/shard_map/ppermute | solution.py:29
  139.2 25.2 %collective-permute-start.19 = (bf16[3,320,256]{2,1,0:T(8,128)(2,1)}, bf16[3,320,256]{2,1,0:T(8,128)(2,1)S(1)}, u32[]{:S(2)}, u32[]{:S(2)}) collective-permute-start(bf16[3,320,256]{2,1,0:T(8,128)(2,1)} %collective-permute-done.18), channel_id=1, source_target_pairs={{0,8},{1,9},{2,10},{3,11},{4,12},{5,13},{6,14},{7,15},{8,64},{9,65... | collective-permute-start | bytes 1474568 | tf_op jit(solution)/shard_map/ppermute | solution.py:29
  140.2 24.6 %collective-permute-start.21 = (bf16[3,320,256]{2,1,0:T(8,128)(2,1)}, bf16[3,320,256]{2,1,0:T(8,128)(2,1)S(1)}, u32[]{:S(2)}, u32[]{:S(2)}) collective-permute-start(bf16[3,320,256]{2,1,0:T(8,128)(2,1)} %collective-permute-done.20), channel_id=1, source_target_pairs={{0,72},{1,73},{2,74},{3,75},{4,76},{5,77},{6,78},{7,79},{8,0},{9,1... | collective-permute-start | bytes 1474568 | tf_op jit(solution)/shard_map/ppermute | solution.py:29
  143.9 15.2 %collective-permute-start.27 = (bf16[2,320,256]{2,1,0:T(8,128)(2,1)}, bf16[2,320,256]{2,1,0:T(8,128)(2,1)S(1)}, u32[]{:S(2)}, u32[]{:S(2)}) collective-permute-start(bf16[2,320,256]{2,1,0:T(8,128)(2,1)} %get-tuple-element.106), channel_id=1, source_target_pairs={{0,8},{1,9},{2,10},{3,11},{4,12},{5,13},{6,14},{7,15},{8,64},{9,65... | collective-permute-start | bytes 983048 | tf_op jit(solution)/shard_map/ppermute | solution.py:29
  143.9 17.5 %collective-permute-start.29 = (bf16[2,320,256]{2,1,0:T(8,128)(2,1)}, bf16[2,320,256]{2,1,0:T(8,128)(2,1)S(1)}, u32[]{:S(2)}, u32[]{:S(2)}) collective-permute-start(bf16[2,320,256]{2,1,0:T(8,128)(2,1)} %get-tuple-element.107), channel_id=1, source_target_pairs={{0,72},{1,73},{2,74},{3,75},{4,76},{5,77},{6,78},{7,79},{8,0},{9,1... | collective-permute-start | bytes 983048 | tf_op jit(solution)/shard_map/ppermute | solution.py:29
  154.3 14.9 %collective-permute-start.26 = (bf16[64,2560]{1,0:T(8,128)(2,1)S(1)}, bf16[64,2560]{1,0:T(8,128)(2,1)S(1)}, u32[]{:S(2)}, u32[]{:S(2)}) collective-permute-start(bf16[64,2560]{1,0:T(8,128)(2,1)S(1)} %get-tuple-element.116), channel_id=1, source_target_pairs={{0,8},{1,9},{2,10},{3,11},{4,12},{5,13},{6,14},{7,15},{8,0},{9,1},... | collective-permute-start | bytes 983048 | tf_op jit(solution)/shard_map/ppermute | solution.py:29
  (23 other events, 198.6 us)
Sparse Core Ops, SparseCore 0:
  26.8 73.1 all-gather.2

commit v3 on v2

--- a/solution.py
+++ b/solution.py
@@ -255,7 +255,7 @@
         out_specs=outs,
         out_shape=shapes,
         compiler_params=ROOM,
-        cost_estimate=lasting(1.5 + 1.8 * steps),
+        cost_estimate=lasting(2 + 2.4 * steps),
     )(columns, *pieces)
 
 
@@ -324,10 +324,9 @@
     front, rear, next_left, last_left, own_left = small(split_left_kernel, outs, keep, send)
     front, rear = moved(front, x=1), moved(rear, x=-1)
 
-    kept_1, *sent = weight("both", after(columns, own_left), pieces[1])
+    sides = small(join_kernel, [like(64, 2560)] * 2, next_left, last_left, front, rear)
+    kept_1, *sent = weight("both", after(columns, *sides), pieces[1])
     other = [moved(after(rows, kept_1), y=way) for rows, way in zip(hop, (1, -1))]
-    next_left = after(next_left, *sent)
-    sides = small(join_kernel, [like(64, 2560)] * 2, next_left, last_left, front, rear)
     right_keep, right_send = small(
         right_sum_kernel, [like(64, 2560, kind=F32), like(64, 2560)], after(own_right, *sent), ahead, behind
     )

time: 181 us -> 185 us (1.022)
  waiting for transfers between devices: 50.2 us -> 55.2 us
    ppermute x31, waiting for transfers between devices: 50.2 us -> 55.2 us  [moved(): return lax.ppermute(value, AXES, pairs)]
  transfers between devices with their start and end apart: 32 -> 32, of which waited for: 13 -> 13; matrix products, arithmetic and copies ran while one was open for 0% -> 0% of each run, Pallas kernels for 35% -> 34%
where the time goes in v3:
time: 185 us
  Pallas kernels  68.8 us (37%)
  waiting for transfers between devices  55.2 us (30%)
  starting transfers between devices  43.9 us (24%)
  between operations  14.2 us (8%)
    ppermute x31, waiting for transfers between devices, moved(): return lax.ppermute(value, AXES, pairs)  55.2 us
    ppermute x31, starting transfers between devices, moved(): return lax.ppermute(value, AXES, pairs)  43.9 us
    pallas_call x2, Pallas kernels, weight(): pl.pallas_call(functools.partial(weight_kernel, task), grid=(steps,), in_...  25.9 us
    pallas_call x2, Pallas kernels, back(): pl.pallas_call(back_kernel, grid=(5,), in_specs=[pl.BlockSpec((1024, 1280...  22.1 us
    pallas_call x1, Pallas kernels, grad_pre_of(): pl.pallas_call(slope_kernel, grid_spec=pltpu.PrefetchScalarGridSpec(num_s...  8.06 us
    pallas_call x6, Pallas kernels, small(): pl.pallas_call(kernel, grid=(1,), in_specs=[pl.BlockSpec(value.shape, lam...  4.01 us
  transfers between devices with their start and end apart: 32, of which 13 were waited for; matrix products, arithmetic and copies ran while one was open for 0% of the time, Pallas kernels for 34%

profile of v3, /device:TPU:0, one launch (start us, length us, event | category | flops | bytes accessed | tf_op | source)
XLA Modules:
  0.0 184.9 jit_solution(10286677813248441084)
XLA Ops:
  7.8 3.1 %shard_map.77 = (bf16[64,1280]{1,0:T(8,128)(2,1)}, bf16[64,1280]{1,0:T(8,128)(2,1)}, bf16[64,1280]{1,0:T(8,128)(2,1)}, bf16[64,1280]{1,0:T(8,128)(2,1)}) custom-call(s32[8]{0:T(128)} %fusion.15.starts, bf16[64,5120]{1,0:T(8,128)(2,1)} %rows_ref.3, f32[1,5120]{1,0:T(1,128)} %bitcast.2), custom_call_target="tpu_custom_call" | custom-call | flops 660000000 | bytes 65536 | tf_op jit(solution)/shard_map/pallas_call | solution.py:73
  10.9 4.1 %collective-permute-start = (bf16[64,1280]{1,0:T(8,128)(2,1)}, bf16[64,1280]{1,0:T(8,128)(2,1)S(1)}, u32[]{:S(2)}, u32[]{:S(2)}) collective-permute-start(bf16[64,1280]{1,0:T(8,128)(2,1)} %get-tuple-element.62), channel_id=1, source_target_pairs={{0,48},{1,49},{2,50},{3,51},{4,52},{5,53},{6,54},{7,55},{8,56},{9,... | collective-permute-start | bytes 491528 | tf_op jit(solution)/shard_map/ppermute | solution.py:29
  16.8 8.1 %shard_map.78 = (bf16[3,1024,256]{2,1,0:T(8,128)(2,1)}, bf16[2,1024,256]{2,1,0:T(8,128)(2,1)}, bf16[1024,1280]{1,0:T(8,128)(2,1)}) custom-call(s32[16]{0:T(128)} %fusion.places, bf16[1024,1280]{1,0:T(8,128)(2,1)} %pre_ref.1, bf16[1024,1280]{1,0:T(8,128)(2,1)} %hidden_ref.1), custom_call_target="tpu_custom_call" | custom-call | flops 2750000128 | bytes 65536 | tf_op jit(solution)/shard_map/pallas_call | solution.py:117
  28.8 10.9 %shard_map.80 = (bf16[512,2560]{1,0:T(8,128)(2,1)}, bf16[256,2560]{1,0:T(8,128)(2,1)}, bf16[256,2560]{1,0:T(8,128)(2,1)}) custom-call(bf16[1024,1280]{1,0:T(8,128)(2,1)} %get-tuple-element.68.rows_ref, bf16[5120,1280]{1,0:T(8,128)(2,1)} %w_ref.3), custom_call_target="tpu_custom_call" | custom-call | flops 550000000 | bytes 65536 | tf_op jit(solution)/shard_map/pallas_call | solution.py:141
  40.2 11.2 %shard_map.81 = (bf16[512,2560]{1,0:T(8,128)(2,1)}, bf16[256,2560]{1,0:T(8,128)(2,1)}, bf16[256,2560]{1,0:T(8,128)(2,1)}) custom-call(bf16[1024,1280]{1,0:T(8,128)(2,1)} %get-tuple-element.68.rows_ref, bf16[5120,1280]{1,0:T(8,128)(2,1)} %w_ref.3), custom_call_target="tpu_custom_call" | custom-call | flops 550000000 | bytes 65536 | tf_op jit(solution)/shard_map/pallas_call | solution.py:141
  51.4 11.7 %collective-permute-done.3.refs_1_ = bf16[3,1024,256]{2,1,0:T(8,128)(2,1)} collective-permute-done((bf16[3,1024,256]{2,1,0:T(8,128)(2,1)}, bf16[3,1024,256]{2,1,0:T(8,128)(2,1)}, u32[]{:S(2)}, u32[]{:S(2)}) %collective-permute-start.3) | collective-permute-done | bytes 1572896 | tf_op jit(solution)/shard_map/ppermute | solution.py:29
  63.0 1.8 collective-permute-done.4.refs_3_
  66.2 3.2 %collective-permute-start.9 = (bf16[2,1024,256]{2,1,0:T(8,128)(2,1)}, bf16[2,1024,256]{2,1,0:T(8,128)(2,1)}, u32[]{:S(2)}, u32[]{:S(2)}) collective-permute-start(bf16[2,1024,256]{2,1,0:T(8,128)(2,1)} %get-tuple-element.104.refs_0_), channel_id=1, source_target_pairs={{0,48},{1,49},{2,50},{3,51},{4,52},{5,53},{6,54},{7,55},{8,56},{9,... | collective-permute-start | bytes 3145736 | tf_op jit(solution)/shard_map/ppermute | solution.py:29
  72.6 1.9 %shard_map.83 = (bf16[256,2560]{1,0:T(8,128)(2,1)S(1)}, bf16[256,2560]{1,0:T(8,128)(2,1)}) custom-call(bf16[512,2560]{1,0:T(8,128)(2,1)S(1)} %copy-done, bf16[256,2560]{1,0:T(8,128)(2,1)S(1)} %collective-permute-done.7.refs_0_, bf16[256,2560]{1,0:T(8,128)(2,1)S(1)} %collective-permute-done.8.refs_1_), custom_call_target="tpu_custom_call" | custom-call | flops 550000000 | bytes 65536 | tf_op jit(solution)/shard_map/pallas_call | solution.py:173
  76.2 8.9 %collective-permute-done.10.front_ref = bf16[64,2560]{1,0:T(8,128)(2,1)S(1)} collective-permute-done((bf16[64,2560]{1,0:T(8,128)(2,1)S(1)}, bf16[64,2560]{1,0:T(8,128)(2,1)S(1)}, u32[]{:S(2)}, u32[]{:S(2)}) %collective-permute-start.10) | collective-permute-done | bytes 327712 | tf_op jit(solution)/shard_map/ppermute | solution.py:29
  85.0 2.4 %collective-permute-done.11.rear_ref = bf16[64,2560]{1,0:T(8,128)(2,1)S(1)} collective-permute-done((bf16[64,2560]{1,0:T(8,128)(2,1)S(1)}, bf16[64,2560]{1,0:T(8,128)(2,1)S(1)}, u32[]{:S(2)}, u32[]{:S(2)}) %collective-permute-start.11) | collective-permute-done | bytes 327712 | tf_op jit(solution)/shard_map/ppermute | solution.py:29
  90.9 3.5 %collective-permute-start.15 = (bf16[2,1024,256]{2,1,0:T(8,128)(2,1)}, bf16[2,1024,256]{2,1,0:T(8,128)(2,1)}, u32[]{:S(2)}, u32[]{:S(2)}) collective-permute-start(bf16[2,1024,256]{2,1,0:T(8,128)(2,1)} %collective-permute-done.9.refs_1_), channel_id=1, source_target_pairs={{0,48},{1,49},{2,50},{3,51},{4,52},{5,53},{6,54},{7,55},{8,56},{9,... | collective-permute-start | bytes 3145736 | tf_op jit(solution)/shard_map/ppermute | solution.py:29
  94.4 8.2 %collective-permute-done.14.refs_2_ = bf16[3,1024,256]{2,1,0:T(8,128)(2,1)S(1)} collective-permute-done((bf16[3,1024,256]{2,1,0:T(8,128)(2,1)}, bf16[3,1024,256]{2,1,0:T(8,128)(2,1)S(1)}, u32[]{:S(2)}, u32[]{:S(2)}) %collective-permute-start.14) | collective-permute-done | bytes 1572896 | tf_op jit(solution)/shard_map/ppermute | solution.py:29
  102.6 3.3 %collective-permute-done.12.ahead_ref = bf16[128,2560]{1,0:T(8,128)(2,1)S(1)} collective-permute-done((bf16[128,2560]{1,0:T(8,128)(2,1)S(1)}, bf16[128,2560]{1,0:T(8,128)(2,1)S(1)}, u32[]{:S(2)}, u32[]{:S(2)}) %collective-permute-start.12) | collective-permute-done | bytes 655392 | tf_op jit(solution)/shard_map/ppermute | solution.py:29
  108.9 14.4 %shard_map.85 = (bf16[3,640,256]{2,1,0:T(8,128)(2,1)}, bf16[3,320,256]{2,1,0:T(8,128)(2,1)}, bf16[3,320,256]{2,1,0:T(8,128)(2,1)}) custom-call(bf16[16,1280,256]{2,1,0:T(8,128)(2,1)} %bitcast.4, bf16[3,1024,256]{2,1,0:T(8,128)(2,1)} %get-tuple-element.70.refs_0_, bf16[3,1024,256]{2,1,0:T(8,128)(2,1)} %collective-permute-done.3.refs_1_, ...), custom_call_target="tpu_custom_call" | custom-call | flops 5059999744 | bytes 65536 | tf_op jit(solution)/shard_map/pallas_call | solution.py:250
  125.1 1.8 collective-permute-start.18
  128.3 1.8 collective-permute-start.22
  130.5 11.5 %shard_map.88 = (bf16[2,640,256]{2,1,0:T(8,128)(2,1)}, bf16[2,320,256]{2,1,0:T(8,128)(2,1)}, bf16[2,320,256]{2,1,0:T(8,128)(2,1)}) custom-call(bf16[16,1280,256]{2,1,0:T(8,128)(2,1)} %bitcast.5, bf16[2,1024,256]{2,1,0:T(8,128)(2,1)} %get-tuple-element.104.refs_0_, bf16[2,1024,256]{2,1,0:T(8,128)(2,1)} %collective-permute-done.9.refs_1_, ...), custom_call_target="tpu_custom_call" | custom-call | flops 3740000000 | bytes 65536 | tf_op jit(solution)/shard_map/pallas_call | solution.py:250
  143.6 1.8 collective-permute-start.23
  145.6 3.0 %collective-permute-start.29 = (bf16[2,320,256]{2,1,0:T(8,128)(2,1)}, bf16[2,320,256]{2,1,0:T(8,128)(2,1)S(1)}, u32[]{:S(2)}, u32[]{:S(2)}) collective-permute-start(bf16[2,320,256]{2,1,0:T(8,128)(2,1)} %get-tuple-element.111), channel_id=1, source_target_pairs={{0,72},{1,73},{2,74},{3,75},{4,76},{5,77},{6,78},{7,79},{8,0},{9,1... | collective-permute-start | bytes 983048 | tf_op jit(solution)/shard_map/ppermute | solution.py:29
  150.2 10.9 %collective-permute-done.27 = bf16[2,320,256]{2,1,0:T(8,128)(2,1)S(1)} collective-permute-done((bf16[2,320,256]{2,1,0:T(8,128)(2,1)}, bf16[2,320,256]{2,1,0:T(8,128)(2,1)S(1)}, u32[]{:S(2)}, u32[]{:S(2)}) %collective-permute-start.27) | collective-permute-done | bytes 327712 | tf_op jit(solution)/shard_map/ppermute | solution.py:29
  161.1 3.0 %collective-permute-start.25 = (bf16[64,2560]{1,0:T(8,128)(2,1)S(1)}, bf16[64,2560]{1,0:T(8,128)(2,1)S(1)}, u32[]{:S(2)}, u32[]{:S(2)}) collective-permute-start(bf16[64,2560]{1,0:T(8,128)(2,1)S(1)} %get-tuple-element.102), channel_id=1, source_target_pairs={{0,6},{1,7},{2,0},{3,1},{4,2},{5,3},{6,4},{7,5},{8,14},{9,15},{10,... | collective-permute-start | bytes 983048 | tf_op jit(solution)/shard_map/ppermute | solution.py:29
  169.3 4.4 %collective-permute-done.26.send_ref = bf16[64,2560]{1,0:T(8,128)(2,1)S(1)} collective-permute-done((bf16[64,2560]{1,0:T(8,128)(2,1)S(1)}, bf16[64,2560]{1,0:T(8,128)(2,1)S(1)}, u32[]{:S(2)}, u32[]{:S(2)}) %collective-permute-start.26) | collective-permute-done | bytes 327712 | tf_op jit(solution)/shard_map/ppermute | solution.py:29
  173.7 2.1 %shard_map.91 = bf16[64,5120]{1,0:T(8,128)(2,1)} custom-call(bf16[64,5120]{1,0:T(8,128)(2,1)S(1)} %copy-done.3, f32[1,5120]{1,0:T(1,128)S(1)} %bitcast.3, bf16[64,5120]{1,0:T(8,128)(2,1)S(1)} %copy-done.4, bf16[64,2560]{1,0:T(8,128)(2,1)S(1)} %get-tuple-element.109.own_ref, bf16[64,2560]{1,0:T(8,128)(2,1)S(1)} %collective-permute-done.24.ahead_ref, ...), custom_call_target="tpu_custom_call" | custom-call | flops 660000000 | bytes 65536 | tf_op jit(solution)/shard_map/pallas_call | solution.py:45
  (87 shorter events, 34.0 us)
Async XLA Ops:
  7.2 101.7 %all-gather.3.cloned.1.call-start = ((), (), s32[]{:S(2)}) async-start(), calls=%async_computation | async-start | bytes 11141120 | tf_op jit(solution)/shard_map/all_gather | solution.py:296
  10.9 14.0 %collective-permute-start = (bf16[64,1280]{1,0:T(8,128)(2,1)}, bf16[64,1280]{1,0:T(8,128)(2,1)S(1)}, u32[]{:S(2)}, u32[]{:S(2)}) collective-permute-start(bf16[64,1280]{1,0:T(8,128)(2,1)} %get-tuple-element.62), channel_id=1, source_target_pairs={{0,48},{1,49},{2,50},{3,51},{4,52},{5,53},{6,54},{7,55},{8,56},{9,... | collective-permute-start | bytes 491528 | tf_op jit(solution)/shard_map/ppermute | solution.py:29
  26.7 36.4 %collective-permute-start.3 = (bf16[3,1024,256]{2,1,0:T(8,128)(2,1)}, bf16[3,1024,256]{2,1,0:T(8,128)(2,1)}, u32[]{:S(2)}, u32[]{:S(2)}) collective-permute-start(bf16[3,1024,256]{2,1,0:T(8,128)(2,1)} %get-tuple-element.70.refs_0_), channel_id=1, source_target_pairs={{0,48},{1,49},{2,50},{3,51},{4,52},{5,53},{6,54},{7,55},{8,56},{9,... | collective-permute-start | bytes 4718600 | tf_op jit(solution)/shard_map/ppermute | solution.py:29
  28.0 36.8 %collective-permute-start.4 = (bf16[3,1024,256]{2,1,0:T(8,128)(2,1)}, bf16[3,1024,256]{2,1,0:T(8,128)(2,1)}, u32[]{:S(2)}, u32[]{:S(2)}) collective-permute-start(bf16[3,1024,256]{2,1,0:T(8,128)(2,1)} %get-tuple-element.70.refs_0_), channel_id=1, source_target_pairs={{0,16},{1,17},{2,18},{3,19},{4,20},{5,21},{6,22},{7,23},{8,24},{9,... | collective-permute-start | bytes 4718600 | tf_op jit(solution)/shard_map/ppermute | solution.py:29
  39.7 25.2 %collective-permute-start.5 = (bf16[256,2560]{1,0:T(8,128)(2,1)}, bf16[256,2560]{1,0:T(8,128)(2,1)S(1)}, u32[]{:S(2)}, u32[]{:S(2)}) collective-permute-start(bf16[256,2560]{1,0:T(8,128)(2,1)} %get-tuple-element.72), channel_id=1, source_target_pairs={{0,1},{1,0},{2,3},{3,2},{4,5},{5,4},{6,7},{7,6},{8,9},{9,8},{10,11... | collective-permute-start | bytes 3932168 | tf_op jit(solution)/shard_map/ppermute | solution.py:29
  39.7 25.2 %collective-permute-start.6 = (bf16[256,2560]{1,0:T(8,128)(2,1)}, bf16[256,2560]{1,0:T(8,128)(2,1)S(1)}, u32[]{:S(2)}, u32[]{:S(2)}) collective-permute-start(bf16[256,2560]{1,0:T(8,128)(2,1)} %get-tuple-element.73), channel_id=1, source_target_pairs={{0,1},{1,0},{2,3},{3,2},{4,5},{5,4},{6,7},{7,6},{8,9},{9,8},{10,11... | collective-permute-start | bytes 3932168 | tf_op jit(solution)/shard_map/ppermute | solution.py:29
  51.4 19.5 %collective-permute-start.7 = (bf16[256,2560]{1,0:T(8,128)(2,1)}, bf16[256,2560]{1,0:T(8,128)(2,1)S(1)}, u32[]{:S(2)}, u32[]{:S(2)}) collective-permute-start(bf16[256,2560]{1,0:T(8,128)(2,1)} %get-tuple-element.76), channel_id=1, source_target_pairs={{0,1},{1,0},{2,3},{3,2},{4,5},{5,4},{6,7},{7,6},{8,9},{9,8},{10,11... | collective-permute-start | bytes 3932168 | tf_op jit(solution)/shard_map/ppermute | solution.py:29
  66.1 36.5 %collective-permute-start.14 = (bf16[3,1024,256]{2,1,0:T(8,128)(2,1)}, bf16[3,1024,256]{2,1,0:T(8,128)(2,1)S(1)}, u32[]{:S(2)}, u32[]{:S(2)}) collective-permute-start(bf16[3,1024,256]{2,1,0:T(8,128)(2,1)} %collective-permute-done.4.refs_3_), channel_id=1, source_target_pairs={{0,16},{1,17},{2,18},{3,19},{4,20},{5,21},{6,22},{7,23},{8,24},{9,... | collective-permute-start | bytes 4718600 | tf_op jit(solution)/shard_map/ppermute | solution.py:29
  66.2 24.7 %collective-permute-start.9 = (bf16[2,1024,256]{2,1,0:T(8,128)(2,1)}, bf16[2,1024,256]{2,1,0:T(8,128)(2,1)}, u32[]{:S(2)}, u32[]{:S(2)}) collective-permute-start(bf16[2,1024,256]{2,1,0:T(8,128)(2,1)} %get-tuple-element.104.refs_0_), channel_id=1, source_target_pairs={{0,48},{1,49},{2,50},{3,51},{4,52},{5,53},{6,54},{7,55},{8,56},{9,... | collective-permute-start | bytes 3145736 | tf_op jit(solution)/shard_map/ppermute | solution.py:29
  69.4 15.6 %collective-permute-start.10 = (bf16[64,2560]{1,0:T(8,128)(2,1)S(1)}, bf16[64,2560]{1,0:T(8,128)(2,1)S(1)}, u32[]{:S(2)}, u32[]{:S(2)}) collective-permute-start(bf16[64,2560]{1,0:T(8,128)(2,1)S(1)} %get-tuple-element.84), channel_id=1, source_target_pairs={{0,2},{1,3},{2,4},{3,5},{4,6},{5,7},{6,0},{7,1},{8,10},{9,11},{10,... | collective-permute-start | bytes 983048 | tf_op jit(solution)/shard_map/ppermute | solution.py:29
  70.9 16.5 %collective-permute-start.11 = (bf16[64,2560]{1,0:T(8,128)(2,1)S(1)}, bf16[64,2560]{1,0:T(8,128)(2,1)S(1)}, u32[]{:S(2)}, u32[]{:S(2)}) collective-permute-start(bf16[64,2560]{1,0:T(8,128)(2,1)S(1)} %get-tuple-element.85), channel_id=1, source_target_pairs={{0,6},{1,7},{2,0},{3,1},{4,2},{5,3},{6,4},{7,5},{8,14},{9,15},{10,... | collective-permute-start | bytes 983048 | tf_op jit(solution)/shard_map/ppermute | solution.py:29
  74.6 48.6 %collective-permute-start.16 = (bf16[256,2560]{1,0:T(8,128)(2,1)}, bf16[256,2560]{1,0:T(8,128)(2,1)S(1)}, u32[]{:S(2)}, u32[]{:S(2)}) collective-permute-start(bf16[256,2560]{1,0:T(8,128)(2,1)} %get-tuple-element.94), channel_id=1, source_target_pairs={{0,8},{1,9},{2,10},{3,11},{4,12},{5,13},{6,14},{7,15},{8,0},{9,1},... | collective-permute-start | bytes 3932168 | tf_op jit(solution)/shard_map/ppermute | solution.py:29
  87.6 18.3 %collective-permute-start.12 = (bf16[128,2560]{1,0:T(8,128)(2,1)S(1)}, bf16[128,2560]{1,0:T(8,128)(2,1)S(1)}, u32[]{:S(2)}, u32[]{:S(2)}) collective-permute-start(bf16[128,2560]{1,0:T(8,128)(2,1)S(1)} %get-tuple-element.86), channel_id=1, source_target_pairs={{0,2},{1,3},{2,4},{3,5},{4,6},{5,7},{6,0},{7,1},{8,10},{9,11},{10,... | collective-permute-start | bytes 1966088 | tf_op jit(solution)/shard_map/ppermute | solution.py:29
  89.2 18.9 %collective-permute-start.13 = (bf16[128,2560]{1,0:T(8,128)(2,1)S(1)}, bf16[128,2560]{1,0:T(8,128)(2,1)S(1)}, u32[]{:S(2)}, u32[]{:S(2)}) collective-permute-start(bf16[128,2560]{1,0:T(8,128)(2,1)S(1)} %get-tuple-element.87), channel_id=1, source_target_pairs={{0,6},{1,7},{2,0},{3,1},{4,2},{5,3},{6,4},{7,5},{8,14},{9,15},{10,... | collective-permute-start | bytes 1966088 | tf_op jit(solution)/shard_map/ppermute | solution.py:29
  90.9 32.3 %collective-permute-start.15 = (bf16[2,1024,256]{2,1,0:T(8,128)(2,1)}, bf16[2,1024,256]{2,1,0:T(8,128)(2,1)}, u32[]{:S(2)}, u32[]{:S(2)}) collective-permute-start(bf16[2,1024,256]{2,1,0:T(8,128)(2,1)} %collective-permute-done.9.refs_1_), channel_id=1, source_target_pairs={{0,48},{1,49},{2,50},{3,51},{4,52},{5,53},{6,54},{7,55},{8,56},{9,... | collective-permute-start | bytes 3145736 | tf_op jit(solution)/shard_map/ppermute | solution.py:29
  102.6 27.9 %collective-permute-start.19 = (bf16[2,1024,256]{2,1,0:T(8,128)(2,1)}, bf16[2,1024,256]{2,1,0:T(8,128)(2,1)}, u32[]{:S(2)}, u32[]{:S(2)}) collective-permute-start(bf16[2,1024,256]{2,1,0:T(8,128)(2,1)} %get-tuple-element.104.refs_0_), channel_id=1, source_target_pairs={{0,16},{1,17},{2,18},{3,19},{4,20},{5,21},{6,22},{7,23},{8,24},{9,... | collective-permute-start | bytes 3145736 | tf_op jit(solution)/shard_map/ppermute | solution.py:29
  126.9 15.2 %collective-permute-start.20 = (bf16[3,320,256]{2,1,0:T(8,128)(2,1)S(1)}, bf16[3,320,256]{2,1,0:T(8,128)(2,1)S(1)}, u32[]{:S(2)}, u32[]{:S(2)}) collective-permute-start(bf16[3,320,256]{2,1,0:T(8,128)(2,1)S(1)} %copy-done.13), channel_id=1, source_target_pairs={{0,8},{1,9},{2,10},{3,11},{4,12},{5,13},{6,14},{7,15},{8,64},{9,65... | collective-permute-start | bytes 1474568 | tf_op jit(solution)/shard_map/ppermute | solution.py:29
  128.3 15.3 %collective-permute-start.22 = (bf16[3,320,256]{2,1,0:T(8,128)(2,1)}, bf16[3,320,256]{2,1,0:T(8,128)(2,1)S(1)}, u32[]{:S(2)}, u32[]{:S(2)}) collective-permute-start(bf16[3,320,256]{2,1,0:T(8,128)(2,1)} %get-tuple-element.91), channel_id=1, source_target_pairs={{0,72},{1,73},{2,74},{3,75},{4,76},{5,77},{6,78},{7,79},{8,0},{9,1... | collective-permute-start | bytes 1474568 | tf_op jit(solution)/shard_map/ppermute | solution.py:29
  142.1 22.3 %collective-permute-start.21 = (bf16[3,320,256]{2,1,0:T(8,128)(2,1)S(1)}, bf16[3,320,256]{2,1,0:T(8,128)(2,1)S(1)}, u32[]{:S(2)}, u32[]{:S(2)}) collective-permute-start(bf16[3,320,256]{2,1,0:T(8,128)(2,1)S(1)} %collective-permute-done.20), channel_id=1, source_target_pairs={{0,8},{1,9},{2,10},{3,11},{4,12},{5,13},{6,14},{7,15},{8,64},{9,65... | collective-permute-start | bytes 1474568 | tf_op jit(solution)/shard_map/ppermute | solution.py:29
  143.6 22.5 %collective-permute-start.23 = (bf16[3,320,256]{2,1,0:T(8,128)(2,1)S(1)}, bf16[3,320,256]{2,1,0:T(8,128)(2,1)S(1)}, u32[]{:S(2)}, u32[]{:S(2)}) collective-permute-start(bf16[3,320,256]{2,1,0:T(8,128)(2,1)S(1)} %collective-permute-done.22), channel_id=1, source_target_pairs={{0,72},{1,73},{2,74},{3,75},{4,76},{5,77},{6,78},{7,79},{8,0},{9,1... | collective-permute-start | bytes 1474568 | tf_op jit(solution)/shard_map/ppermute | solution.py:29
  145.4 15.8 %collective-permute-start.27 = (bf16[2,320,256]{2,1,0:T(8,128)(2,1)}, bf16[2,320,256]{2,1,0:T(8,128)(2,1)S(1)}, u32[]{:S(2)}, u32[]{:S(2)}) collective-permute-start(bf16[2,320,256]{2,1,0:T(8,128)(2,1)} %get-tuple-element.110), channel_id=1, source_target_pairs={{0,8},{1,9},{2,10},{3,11},{4,12},{5,13},{6,14},{7,15},{8,64},{9,65... | collective-permute-start | bytes 983048 | tf_op jit(solution)/shard_map/ppermute | solution.py:29
  145.6 18.5 %collective-permute-start.29 = (bf16[2,320,256]{2,1,0:T(8,128)(2,1)}, bf16[2,320,256]{2,1,0:T(8,128)(2,1)S(1)}, u32[]{:S(2)}, u32[]{:S(2)}) collective-permute-start(bf16[2,320,256]{2,1,0:T(8,128)(2,1)} %get-tuple-element.111), channel_id=1, source_target_pairs={{0,72},{1,73},{2,74},{3,75},{4,76},{5,77},{6,78},{7,79},{8,0},{9,1... | collective-permute-start | bytes 983048 | tf_op jit(solution)/shard_map/ppermute | solution.py:29
  148.6 20.7 %collective-permute-start.24 = (bf16[64,2560]{1,0:T(8,128)(2,1)S(1)}, bf16[64,2560]{1,0:T(8,128)(2,1)S(1)}, u32[]{:S(2)}, u32[]{:S(2)}) collective-permute-start(bf16[64,2560]{1,0:T(8,128)(2,1)S(1)} %get-tuple-element.101), channel_id=1, source_target_pairs={{0,2},{1,3},{2,4},{3,5},{4,6},{5,7},{6,0},{7,1},{8,10},{9,11},{10,... | collective-permute-start | bytes 983048 | tf_op jit(solution)/shard_map/ppermute | solution.py:29
  164.4 11.4 %collective-permute-start.28 = (bf16[2,320,256]{2,1,0:T(8,128)(2,1)S(1)}, bf16[2,320,256]{2,1,0:T(8,128)(2,1)S(1)}, u32[]{:S(2)}, u32[]{:S(2)}) collective-permute-start(bf16[2,320,256]{2,1,0:T(8,128)(2,1)S(1)} %collective-permute-done.27), channel_id=1, source_target_pairs={{0,8},{1,9},{2,10},{3,11},{4,12},{5,13},{6,14},{7,15},{8,64},{9,65... | collective-permute-start | bytes 983048 | tf_op jit(solution)/shard_map/ppermute | solution.py:29
  (22 other events, 206.8 us)
Sparse Core Ops, SparseCore 0:
  26.8 73.0 all-gather.2
